TPU v7x, 32 devices: a whole 2x2x4 slice. The times are simulated.
32 devices in a mesh: ty: 8 (over y, x, core), tx: 4 (over z).
Axes of the slice: x: 2, y: 2, z: 4, core: 2. Of those that a mesh axis runs over, the one named last changes fastest.
Arguments:
- block_input: bfloat16 [512, 192, 256], P('ty', 'tx'), may hold values from -6 to 6
- cotangent: bfloat16 [512, 192, 256], P('ty', 'tx'), may hold values from -6 to 6
- tissue: int32 [32, 12], P('ty', 'tx'), may hold values 0 or 1
- dw_weight: float32 [49, 256], replicated, may hold values from -0.875 to 0.875
- dw_bias: float32 [256], replicated, may hold values from -3 to 3
- ln_gain: float32 [256], replicated, may hold values from 0.5 to 1.5
- ln_bias: float32 [256], replicated, may hold values from -3 to 3
- w_expand: bfloat16 [256, 1024], replicated, may hold values from -0.375 to 0.375
- b_expand: float32 [1024], replicated, may hold values from -3 to 3
- w_reduce: bfloat16 [1024, 256], replicated, may hold values from -0.1875 to 0.1875
- layer_scale: float32 [256], replicated, may hold values from 0.5 to 2
Outputs:
- grad_input: bfloat16 [512, 192, 256], P('ty', 'tx')
- grad_dw: float32 [49, 256], replicated
- grad_expand: float32 [256, 1024], replicated
- grad_reduce: float32 [1024, 256], replicated
Inputs may be any that keep to these rules, and one draw needn't show every extreme that they name: 1 marks a tile with tissue.
All inputs are finite; a program needn't handle non-finite values. No bound on the sum of `tissue` on one device may be relied on, other than what follows from the above.
Results may differ from a plain program's by a relative error of at most 0.007.
Values may be sent and summed in bfloat16 or wider, within the bound.
A program may use at most 256 MiB of HBM per device.

v0:
```python
import math

import jax
import jax.numpy as jnp
from jax import lax
from jax.sharding import PartitionSpec as P

TILE = 16


def with_halo(block, sides, width):
    for axis, dim in sides:
        count = lax.axis_size(axis)
        forward = [(i, i + 1) for i in range(count - 1)]
        backward = [(target, source) for source, target in forward]
        low = lax.ppermute(
            lax.slice_in_dim(block, block.shape[dim] - width, None, axis=dim), axis, forward
        )
        high = lax.ppermute(lax.slice_in_dim(block, 0, width, axis=dim), axis, backward)
        block = jnp.concatenate([low, block, high], axis=dim)
    return block


def depthwise(padded, kernel, rows, cols):
    total = jnp.zeros((rows, cols, padded.shape[2]), jnp.float32)
    for row_off in range(7):
        for col_off in range(7):
            window = padded[row_off : row_off + rows, col_off : col_off + cols].astype(jnp.float32)
            total = total + window * kernel[row_off * 7 + col_off]
    return total


def filter_grad(padded, grad, rows, cols):
    gradf = grad.astype(jnp.float32)
    taps = []
    for row_off in range(7):
        for col_off in range(7):
            window = padded[row_off : row_off + rows, col_off : col_off + cols].astype(jnp.float32)
            taps.append(jnp.sum(window * gradf, axis=(0, 1)))
    return jnp.stack(taps)


def branch_back(pre, masked, ln_gain, ln_bias, w_expand, b_expand, w_reduce, layer_scale):
    center = pre - jnp.mean(pre, axis=-1, keepdims=True)
    rstd = lax.rsqrt(jnp.mean(center * center, axis=-1, keepdims=True) + 1e-06)
    nhat = center * rstd
    normed = (nhat * ln_gain + ln_bias).astype(jnp.bfloat16)
    zvals = jnp.dot(normed, w_expand, preferred_element_type=jnp.float32) + b_expand
    cdf = 0.5 * (1.0 + jax.scipy.special.erf(zvals * 0.7071067811865476))
    hidden = (zvals * cdf).astype(jnp.bfloat16)
    go_vals = (layer_scale * masked.astype(jnp.float32)).astype(jnp.bfloat16)
    dhid = jnp.dot(go_vals, w_reduce.T, preferred_element_type=jnp.float32)
    slope = cdf + zvals * jnp.exp(-0.5 * zvals * zvals) * 0.3989422804014327
    dzvals = (dhid * slope).astype(jnp.bfloat16)
    dnorm = jnp.dot(dzvals, w_expand.T, preferred_element_type=jnp.float32) * ln_gain
    grad = rstd * (
        dnorm
        - jnp.mean(dnorm, axis=-1, keepdims=True)
        - nhat * jnp.mean(dnorm * nhat, axis=-1, keepdims=True)
    )
    return (grad.astype(jnp.bfloat16), hidden, normed, go_vals, dzvals)


def body(
    block_input,
    cotangent,
    tissue,
    dw_weight,
    dw_bias,
    ln_gain,
    ln_bias,
    w_expand,
    b_expand,
    w_reduce,
    layer_scale,
):
    rows, cols, chans = block_input.shape
    mask = jnp.repeat(jnp.repeat(tissue, TILE, axis=0), TILE, axis=1)
    masked = (cotangent.astype(jnp.float32) * mask[:, :, None].astype(jnp.float32)).astype(
        jnp.bfloat16
    )
    params = (ln_gain, ln_bias, w_expand, b_expand, w_reduce, layer_scale)
    input_pad = with_halo(block_input, (("ty", 0), ("tx", 1)), 3)
    pre = depthwise(input_pad, dw_weight, rows, cols) + dw_bias
    grad, hidden, normed, go_vals, dzvals = branch_back(
        pre.reshape(-1, chans), masked.reshape(-1, chans), *params
    )
    grad_core = grad.reshape(rows, cols, chans)
    grad_pad = with_halo(grad_core, (("ty", 0), ("tx", 1)), 3)
    factor = 1.0 / math.sqrt(rows * lax.axis_size("ty") * cols * lax.axis_size("tx"))
    local_reduce = jnp.dot(hidden.T, go_vals, preferred_element_type=jnp.float32)
    local_expand = jnp.dot(normed.T, dzvals, preferred_element_type=jnp.float32)
    local_dw = filter_grad(input_pad, grad_core, rows, cols)
    total_expand, total_reduce, total_dw = lax.psum(
        (local_expand, local_reduce, local_dw), ("ty", "tx")
    )
    result = cotangent.astype(jnp.float32) + depthwise(grad_pad, dw_weight[::-1], rows, cols)
    return (
        result.astype(jnp.bfloat16),
        total_dw * factor,
        total_expand * factor,
        total_reduce * factor,
    )


def solution(mesh):
    placed = (
        P("ty", "tx", None),
        P("ty", "tx", None),
        P("ty", "tx"),
        P(),
        P(),
        P(),
        P(),
        P(),
        P(),
        P(),
        P(),
    )
    return jax.shard_map(
        body,
        mesh=mesh,
        in_specs=placed,
        out_specs=(P("ty", "tx", None), P(), P(), P()),
        check_vma=False,
    )
```

profile of v0, /device:TPU:0, one launch (start us, length us, event | category | flops | bytes accessed | tf_op | source)
XLA Modules:
  0.0 356.2 jit_solution(7813933674325449258)
XLA Ops:
  8.2 1.3 collective-permute-start.1
  9.5 3.0 collective-permute-start
  14.7 2.0 fusion.8
  16.7 1.6 fusion.132
  20.4 4.9 %collective-permute-start.2 = (bf16[70,3,256]{2,1,0:T(4,128)(2,1)S(1)}, bf16[70,3,256]{2,1,0:T(4,128)(2,1)S(1)}, u32[]{:S(2)}, u32[]{:S(2)}) collective-permute-start(bf16[70,3,256]{2,1,0:T(4,128)(2,1)S(1)} %get-tuple-element.69), channel_id=1, source_target_pairs={{0,1},{1,2},{2,3},{4,5},{5,6},{6,7},{8,9},{9,10},{10,11},{12,13},{... | collective-permute-start | bytes 322568 | tf_op jit(solution)/shard_map/ppermute | solution.py:16
  25.3 1.3 collective-permute-start.3
  26.7 2.6 collective-permute-done.2
  29.3 4.4 %collective-permute-done.3 = bf16[70,3,256]{2,1,0:T(4,128)(2,1)S(1)} collective-permute-done((bf16[70,3,256]{2,1,0:T(4,128)(2,1)S(1)}, bf16[70,3,256]{2,1,0:T(4,128)(2,1)S(1)}, u32[]{:S(2)}, u32[]{:S(2)}) %collective-permute-start.3) | collective-permute-done | bytes 107552 | tf_op jit(solution)/shard_map/ppermute | solution.py:19
  33.7 61.1 %fusion.180 = (f32[64,48]{1,0:T(8,128)S(1)}, f32[64,48,256]{2,1,0:T(8,128)}) fusion(f32[256]{0:T(256)S(1)} %copy-done.23, f32[256]{0:T(256)S(1)} %bitcast.232, bf16[70,3,256]{2,1,0:T(4,128)(2,1)S(1)} %collective-permute-done.3, bf16[70,48,256]{2,1,0:T(8,128)(2,1)} %copy-done.4, f32[256]{0:T(256)S(1)} %bitcast.234, f32[256]{0:T(256)S(1)} %bitcast.140, ...), kind=kLoop, calls=%fused_computation.358 | loop fusion | flops 215479296 | bytes 16154624 | tf_op jit(solution)/shard_map/reduce_sum | solution.py:44
  95.0 2.8 multiply_reduce_fusion.1
  97.9 3.1 add_convert_fusion
  101.1 1.8 fusion.188
  102.9 5.5 %fusion.6 = f32[1024,256]{1,0:T(8,128)} fusion(bf16[3072,256]{1,0:T(8,128)(2,1)S(1)} %copy-done.12, f32[3072,1024]{1,0:T(8,128)S(1)} %fusion.188, f32[1024]{0:T(1024)S(1)} %copy-done.27), kind=kOutput, calls=%fused_computation.99 | convolution fusion | flops 1629487104 | bytes 15208448 | tf_op jit(solution)/shard_map/dot_general | solution.py:91
  108.4 7.0 %fusion.5 = bf16[3072,1024]{1,0:T(8,128)(2,1)S(1)} fusion(f32[3072,1024]{1,0:T(8,128)S(1)} %fusion.188, bf16[3072,256]{1,0:T(8,128)(2,1)S(1)} %copy-done.12, bf16[1024,256]{1,0:T(8,128)(2,1)S(1)} %copy-done.26, f32[1024]{0:T(1024)S(1)} %copy-done.27), kind=kOutput, calls=%fused_computation.96 | convolution fusion | flops 1645215744 | bytes 20975616 | tf_op jit(solution)/shard_map/dot_general | solution.py:52
  115.4 2.7 copy-done.9
  118.0 2.8 fusion.189
  120.8 6.2 %fusion.179 = (f32[3072]{0:T(1024)S(1)}, f32[3072]{0:T(1024)S(1)}, f32[3072,256]{1,0:T(8,128)S(1)}) fusion(f32[3072]{0:T(1024)S(1)} %rsqrt.12, f32[3072]{0:T(1024)S(1)} %div.16, f32[64,48,256]{2,1,0:T(8,128)} %get-tuple-element.64, f32[256]{0:T(256)S(1)} %copy-done.25, bf16[3072,1024]{1,0:T(8,128)(2,1)} %copy-done.9, bf16[256,1024]{1,0:T(8,128)(2,1)S(1)} %copy-done), kind=kOutput, calls=%fused_computation.357 | convolution fusion | flops 1615325184 | bytes 13157376 | tf_op jit(solution)/shard_map/dot_general | solution.py:55
  127.0 2.5 multiply_convert_fusion.2
  130.9 3.0 collective-permute-start.4
  133.9 5.1 %fusion.129 = (f32[256]{0:T(256)S(1)}, f32[256]{0:T(256)S(1)}, f32[256]{0:T(256)S(1)}, f32[256]{0:T(256)S(1)}, f32[256]{0:T(256)S(1)}, /*index=5*/f32[256]{0:T(2...) fusion(bf16[64,48,256]{2,1,0:T(8,128)(2,1)S(1)} %bitcast.126, ...), kind=kLoop, calls=%fused_computation.274 | loop fusion | flops 38532608 | bytes 9809920 | tf_op jit(solution)/shard_map/reduce_sum | solution.py:39
  139.1 6.0 %fusion.131 = (f32[256]{0:T(256)S(1)}, f32[256]{0:T(256)S(1)}, f32[256]{0:T(256)S(1)}, f32[256]{0:T(256)S(1)}, f32[256]{0:T(256)S(1)}, /*index=5*/f32[256]{0:T(2...) fusion(bf16[64,48,256]{2,1,0:T(8,128)(2,1)S(1)} %bitcast.127, bf16[70,3,256]{2,1,0:T(4,128)(2,1)S(1)} %collective-permute-done.3, ...), kind=kLoop, calls=%fused_computation.276 | loop fusion | flops 43251456 | bytes 3409920 | tf_op jit(solution)/shard_map/reduce_sum | solution.py:39
  145.0 6.4 %fusion.130 = (f32[256]{0:T(256)S(1)}, f32[256]{0:T(256)S(1)}, f32[256]{0:T(256)S(1)}, f32[256]{0:T(256)S(1)}, f32[256]{0:T(256)S(1)}, /*index=5*/f32[256]{0:T(2...) fusion(bf16[64,48,256]{2,1,0:T(8,128)(2,1)S(1)} %bitcast.128, bf16[70,3,256]{2,1,0:T(4,128)(2,1)S(1)} %collective-permute-done.3, ...), kind=kLoop, calls=%fused_computation.275 | loop fusion | flops 43251456 | bytes 3409920 | tf_op jit(solution)/shard_map/reduce_sum | solution.py:39
  151.4 5.0 %fusion.126 = (f32[256]{0:T(256)S(1)}, f32[256]{0:T(256)S(1)}, f32[256]{0:T(256)S(1)}, f32[256]{0:T(256)S(1)}, f32[256]{0:T(256)S(1)}, /*index=5*/f32[256]{0:T(2...) fusion(bf16[64,48,256]{2,1,0:T(8,128)(2,1)S(1)} %bitcast.129, bf16[70,48,256]{2,1,0:T(8,128)(2,1)S(1)} %copy-done.5, ...), kind=kLoop, calls=%fused_computation.271 | loop fusion | flops 43251456 | bytes 3409920 | tf_op jit(solution)/shard_map/reduce_sum | solution.py:39
  156.4 5.1 %fusion.127 = (f32[256]{0:T(256)S(1)}, f32[256]{0:T(256)S(1)}, f32[256]{0:T(256)S(1)}, f32[256]{0:T(256)S(1)}, f32[256]{0:T(256)S(1)}, /*index=5*/f32[256]{0:T(2...) fusion(bf16[64,48,256]{2,1,0:T(8,128)(2,1)S(1)} %bitcast.130, bf16[70,48,256]{2,1,0:T(8,128)(2,1)S(1)} %copy-done.5, ...), kind=kLoop, calls=%fused_computation.272 | loop fusion | flops 43251456 | bytes 3409920 | tf_op jit(solution)/shard_map/reduce_sum | solution.py:39
  162.5 41.6 %psum.21 = f32[49,256]{1,0:T(8,128)S(1)} all-reduce(f32[49,256]{1,0:T(8,128)S(1)} %stack.199), channel_id=1, replica_groups=mesh['ty'=8,'tx'=4] {'ty','tx'}, use_global_device_ids=true, to_apply=%region_53.0 | all-reduce | flops 12544 | bytes 100352 | tf_op jit(solution)/shard_map/psum | solution.py:94
  204.3 2.2 collective-permute-start.6
  209.1 4.4 %collective-permute-done.7 = bf16[70,3,256]{2,1,0:T(4,128)(2,1)S(1)} collective-permute-done((bf16[70,3,256]{2,1,0:T(4,128)(2,1)S(1)}, bf16[70,3,256]{2,1,0:T(4,128)(2,1)S(1)}, u32[]{:S(2)}, u32[]{:S(2)}) %collective-permute-start.7) | collective-permute-done | bytes 107552 | tf_op jit(solution)/shard_map/ppermute | solution.py:19
  213.5 2.6 maximum_maximum_fusion
  216.1 33.2 %fusion.9 = bf16[64,48,256]{2,1,0:T(8,128)(2,1)} fusion(bf16[64,48,256]{2,1,0:T(8,128)(2,1)} %param.12, bf16[64,48,256]{2,1,0:T(8,128)(2,1)} %bitcast.134, bf16[3,48,256]{2,1,0:T(8,128)(2,1)S(1)} %collective-permute-done.5, bf16[3,48,256]{2,1,0:T(8,128)(2,1)S(1)} %collective-permute-done.4, bf16[70,51,256]{2,1,0:T(8,128)(2,1)S(1)} %get-tuple-element.66, ...), kind=kLoop, calls=%fused_computation.154 | loop fusion | flops 121896960 | bytes 70976512 | tf_op jit(solution)/shard_map/convert_element_type | solution.py:99
  249.3 95.4 %all-reduce.3.cloned.1.call-done = (f32[256,1024]{1,0:T(8,128)}, f32[1024,256]{1,0:T(8,128)}) async-done(((f32[256,1024]{1,0:T(8,128)}, f32[1024,256]{1,0:T(8,128)}), (f32[256,1024]{1,0:T(8,128)}, f32[1024,256]{1,0:T(8,128)})) %all-reduce.3.cloned.1.call-update) | async-done | bytes 2097168 | tf_op jit(solution)/shard_map/psum | solution.py:94
  344.7 2.3 broadcast_multiply_fusion.1
  347.0 2.3 broadcast_multiply_fusion
  (88 shorter events, 10.4 us)
Async XLA Ops:
  7.2 93.9 %copy-start = (bf16[256,1024]{1,0:T(8,128)(2,1)S(1)}, bf16[256,1024]{1,0:T(8,128)(2,1)}, u32[]{:S(2)}) copy-start(bf16[256,1024]{1,0:T(8,128)(2,1)} %param.18) | copy-start | bytes 1572868
  7.2 9.5 %copy-start.22 = (f32[256]{0:T(256)S(1)}, f32[256]{0:T(256)}, u32[]{:S(2)}) copy-start(f32[256]{0:T(256)} %param.21) | copy-start | bytes 3076
  7.2 337.5 %all-reduce.3.cloned.1.call-start = ((), (), s32[]{:S(2)}) async-start(), calls=%async_computation | async-start | bytes 4194304 | tf_op jit(solution)/shard_map/psum | solution.py:94
  8.2 10.4 %collective-permute-start.1 = (bf16[3,48,256]{2,1,0:T(8,128)(2,1)S(1)}, bf16[3,48,256]{2,1,0:T(8,128)(2,1)S(1)}, u32[]{:S(2)}, u32[]{:S(2)}) collective-permute-start(bf16[3,48,256]{2,1,0:T(8,128)(2,1)S(1)} %get-tuple-element.76), channel_id=1, source_target_pairs={{4,0},{8,4},{12,8},{16,12},{20,16},{24,20},{28,24},{5,1},{9,5},{13... | collective-permute-start | bytes 221192 | tf_op jit(solution)/shard_map/ppermute | solution.py:19
  9.5 8.8 %collective-permute-start = (bf16[3,48,256]{2,1,0:T(8,128)(2,1)S(1)}, bf16[3,48,256]{2,1,0:T(8,128)(2,1)S(1)}, u32[]{:S(2)}, u32[]{:S(2)}) collective-permute-start(bf16[3,48,256]{2,1,0:T(8,128)(2,1)S(1)} %get-tuple-element.77), channel_id=1, source_target_pairs={{0,4},{4,8},{8,12},{12,16},{16,20},{20,24},{24,28},{1,5},{5,9},{9,... | collective-permute-start | bytes 221192 | tf_op jit(solution)/shard_map/ppermute | solution.py:16
  14.6 3.6 %copy-start.13 = (f32[49,256]{1,0:T(8,128)S(1)}, f32[49,256]{1,0:T(8,128)}, u32[]{:S(2)}) copy-start(f32[49,256]{1,0:T(8,128)} %param.14) | copy-start | bytes 150532
  14.6 3.7 %copy-start.10 = (bf16[64,48,256]{2,1,0:T(8,128)(2,1)S(1)}, bf16[64,48,256]{2,1,0:T(8,128)(2,1)}, u32[]{:S(2)}) copy-start(bf16[64,48,256]{2,1,0:T(8,128)(2,1)} %param.11) | copy-start | bytes 4718596
  18.3 15.4 %copy-start.23 = (f32[256]{0:T(256)S(1)}, f32[256]{0:T(256)}, u32[]{:S(2)}) copy-start(f32[256]{0:T(256)} %param.15) | copy-start | bytes 3076
  18.7 76.1 %copy-start.2 = (bf16[67,48,256]{2,1,0:T(8,128)(2,1)}, bf16[67,48,256]{2,1,0:T(8,128)(2,1)S(1)}, u32[]{:S(2)}) copy-start(bf16[67,48,256]{2,1,0:T(8,128)(2,1)S(1)} %get-tuple-element.80) | copy-start | bytes 4939780
  20.4 8.9 %collective-permute-start.2 = (bf16[70,3,256]{2,1,0:T(4,128)(2,1)S(1)}, bf16[70,3,256]{2,1,0:T(4,128)(2,1)S(1)}, u32[]{:S(2)}, u32[]{:S(2)}) collective-permute-start(bf16[70,3,256]{2,1,0:T(4,128)(2,1)S(1)} %get-tuple-element.69), channel_id=1, source_target_pairs={{0,1},{1,2},{2,3},{4,5},{5,6},{6,7},{8,9},{9,10},{10,11},{12,13},{... | collective-permute-start | bytes 322568 | tf_op jit(solution)/shard_map/ppermute | solution.py:16
  25.3 8.4 %collective-permute-start.3 = (bf16[70,3,256]{2,1,0:T(4,128)(2,1)S(1)}, bf16[70,3,256]{2,1,0:T(4,128)(2,1)S(1)}, u32[]{:S(2)}, u32[]{:S(2)}) collective-permute-start(bf16[70,3,256]{2,1,0:T(4,128)(2,1)S(1)} %get-tuple-element.70), channel_id=1, source_target_pairs={{1,0},{2,1},{3,2},{5,4},{6,5},{7,6},{9,8},{10,9},{11,10},{13,12},{... | collective-permute-start | bytes 322568 | tf_op jit(solution)/shard_map/ppermute | solution.py:19
  26.6 68.2 %copy-start.14 = (f32[1,256]{1,0:T(1,128)}, f32[1,256]{1,0:T(1,128)S(1)}, u32[]{:S(2)}) copy-start(f32[1,256]{1,0:T(1,128)S(1)} %get-tuple-element.123) | copy-start | bytes 3076
  26.6 68.2 %copy-start.15 = (f32[1,256]{1,0:T(1,128)}, f32[1,256]{1,0:T(1,128)S(1)}, u32[]{:S(2)}) copy-start(f32[1,256]{1,0:T(1,128)S(1)} %get-tuple-element.124) | copy-start | bytes 3076
  26.6 68.2 %copy-start.16 = (f32[1,256]{1,0:T(1,128)}, f32[1,256]{1,0:T(1,128)S(1)}, u32[]{:S(2)}) copy-start(f32[1,256]{1,0:T(1,128)S(1)} %get-tuple-element.125) | copy-start | bytes 3076
  26.7 68.2 %copy-start.17 = (f32[1,256]{1,0:T(1,128)}, f32[1,256]{1,0:T(1,128)S(1)}, u32[]{:S(2)}) copy-start(f32[1,256]{1,0:T(1,128)S(1)} %get-tuple-element.126) | copy-start | bytes 3076
  26.7 68.2 %copy-start.18 = (f32[1,256]{1,0:T(1,128)}, f32[1,256]{1,0:T(1,128)S(1)}, u32[]{:S(2)}) copy-start(f32[1,256]{1,0:T(1,128)S(1)} %get-tuple-element.127) | copy-start | bytes 3076
  26.7 68.2 %copy-start.19 = (f32[1,256]{1,0:T(1,128)}, f32[1,256]{1,0:T(1,128)S(1)}, u32[]{:S(2)}) copy-start(f32[1,256]{1,0:T(1,128)S(1)} %get-tuple-element.128) | copy-start | bytes 3076
  26.7 68.2 %copy-start.20 = (f32[1,256]{1,0:T(1,128)}, f32[1,256]{1,0:T(1,128)S(1)}, u32[]{:S(2)}) copy-start(f32[1,256]{1,0:T(1,128)S(1)} %get-tuple-element.129) | copy-start | bytes 3076
  26.7 68.2 %copy-start.21 = (f32[1,256]{1,0:T(1,128)}, f32[1,256]{1,0:T(1,128)S(1)}, u32[]{:S(2)}) copy-start(f32[1,256]{1,0:T(1,128)S(1)} %get-tuple-element.130) | copy-start | bytes 3076
  94.9 3.0 copy-start.24
  94.9 3.0 copy-start.25
  102.9 5.5 %copy-start.26 = (bf16[1024,256]{1,0:T(8,128)(2,1)S(1)}, bf16[1024,256]{1,0:T(8,128)(2,1)}, u32[]{:S(2)}) copy-start(bf16[1024,256]{1,0:T(8,128)(2,1)} %param.20) | copy-start | bytes 1572868
  120.8 6.2 %copy-start.8 = (f32[64,48,256]{2,1,0:T(8,128)S(1)}, f32[64,48,256]{2,1,0:T(8,128)}, u32[]{:S(2)}) copy-start(f32[64,48,256]{2,1,0:T(8,128)} %get-tuple-element.64) | copy-start | bytes 9437188
  127.0 6.9 %copy-start.5 = (bf16[70,48,256]{2,1,0:T(8,128)(2,1)S(1)}, bf16[70,48,256]{2,1,0:T(8,128)(2,1)}, u32[]{:S(2)}) copy-start(bf16[70,48,256]{2,1,0:T(8,128)(2,1)} %copy-done.4) | copy-start | bytes 5160964
  127.0 6.9 %copy-start.7 = (bf16[67,48,256]{2,1,0:T(8,128)(2,1)S(1)}, bf16[67,48,256]{2,1,0:T(8,128)(2,1)}, u32[]{:S(2)}) copy-start(bf16[67,48,256]{2,1,0:T(8,128)(2,1)} %copy-done.6) | copy-start | bytes 4939780
  127.0 6.9 %copy-start.11 = (bf16[64,48,256]{2,1,0:T(8,128)(2,1)S(1)}, bf16[64,48,256]{2,1,0:T(8,128)(2,1)}, u32[]{:S(2)}) copy-start(bf16[64,48,256]{2,1,0:T(8,128)(2,1)} %param.11) | copy-start | bytes 4718596
  129.5 74.6 %copy-start.1 = (bf16[3072,256]{1,0:T(8,128)(2,1)}, bf16[3072,256]{1,0:T(8,128)(2,1)S(1)}, u32[]{:S(2)}) copy-start(bf16[3072,256]{1,0:T(8,128)(2,1)S(1)} %multiply_convert_fusion.2) | copy-start | bytes 4718596
  129.6 74.6 %collective-permute-start.5 = (bf16[3,48,256]{2,1,0:T(8,128)(2,1)S(1)}, bf16[3,48,256]{2,1,0:T(8,128)(2,1)S(1)}, u32[]{:S(2)}, u32[]{:S(2)}) collective-permute-start(bf16[3,48,256]{2,1,0:T(8,128)(2,1)S(1)} %bitcast.137), channel_id=1, source_target_pairs={{4,0},{8,4},{12,8},{16,12},{20,16},{24,20},{28,24},{5,1},{9,5},{13... | collective-permute-start | bytes 221192 | tf_op jit(solution)/shard_map/ppermute | solution.py:19
  130.9 73.3 %collective-permute-start.4 = (bf16[3,48,256]{2,1,0:T(8,128)(2,1)S(1)}, bf16[3,48,256]{2,1,0:T(8,128)(2,1)S(1)}, u32[]{:S(2)}, u32[]{:S(2)}) collective-permute-start(bf16[3,48,256]{2,1,0:T(8,128)(2,1)S(1)} %bitcast.136), channel_id=1, source_target_pairs={{0,4},{4,8},{8,12},{12,16},{16,20},{20,24},{24,28},{1,5},{5,9},{9,... | collective-permute-start | bytes 221192 | tf_op jit(solution)/shard_map/ppermute | solution.py:16
  151.4 10.1 %copy-start.3 = (bf16[67,48,256]{2,1,0:T(8,128)(2,1)S(1)}, bf16[67,48,256]{2,1,0:T(8,128)(2,1)}, u32[]{:S(2)}) copy-start(bf16[67,48,256]{2,1,0:T(8,128)(2,1)} %copy-done.2) | copy-start | bytes 4939780
  204.3 4.8 %collective-permute-start.6 = (bf16[70,3,256]{2,1,0:T(4,128)(2,1)S(1)}, bf16[70,3,256]{2,1,0:T(4,128)(2,1)S(1)}, u32[]{:S(2)}, u32[]{:S(2)}) collective-permute-start(bf16[70,3,256]{2,1,0:T(4,128)(2,1)S(1)} %get-tuple-element.67), channel_id=1, source_target_pairs={{0,1},{1,2},{2,3},{4,5},{5,6},{6,7},{8,9},{9,10},{10,11},{12,13},{... | collective-permute-start | bytes 322568 | tf_op jit(solution)/shard_map/ppermute | solution.py:16
  206.5 7.0 %collective-permute-start.7 = (bf16[70,3,256]{2,1,0:T(4,128)(2,1)S(1)}, bf16[70,3,256]{2,1,0:T(4,128)(2,1)S(1)}, u32[]{:S(2)}, u32[]{:S(2)}) collective-permute-start(bf16[70,3,256]{2,1,0:T(4,128)(2,1)S(1)} %get-tuple-element.68), channel_id=1, source_target_pairs={{1,0},{2,1},{3,2},{5,4},{6,5},{7,6},{9,8},{10,9},{11,10},{13,12},{... | collective-permute-start | bytes 322568 | tf_op jit(solution)/shard_map/ppermute | solution.py:19
  (5 other events, 9.3 us)
Sparse Core Ops, SparseCore 0:
  208.5 136.1 all-reduce.2
where the time goes:
time: 357 us; the launch traced here: 356 us
  other arithmetic  143 us (40%)
  waiting for transfers between devices  107 us (30%)
  blocking collectives  41.6 us (12%)
  matrix products  23.2 us (6%)
  starting transfers between devices  18.4 us (5%)
  between operations  14.7 us (4%)
  local copies, waits for them, and re-layouts  7.49 us (2%)
    psum x1, waiting for transfers between devices, body(): lax.psum((local_expand, local_reduce, local_dw), ('ty', 'tx'))  95.4 us
    reduce_sum x1, other arithmetic, branch_back(): center = pre - jnp.mean(pre, axis=-1, keepdims=True)  61.1 us
    psum x1, blocking collectives, body(): lax.psum((local_expand, local_reduce, local_dw), ('ty', 'tx'))  41.6 us
    convert_element_type x1, other arithmetic, body(): result.astype(jnp.bfloat16)  33.2 us
    reduce_sum x6, other arithmetic, filter_grad(): taps.append(jnp.sum(window * gradf, axis=(0, 1)))  28.4 us
    ppermute x4, starting transfers between devices, with_halo(): lax.ppermute(lax.slice_in_dim(block, block.shape[dim] - width, None, axis...  13.2 us
    ppermute x4, waiting for transfers between devices, with_halo(): lax.ppermute(lax.slice_in_dim(block, 0, width, axis=dim), axis, backward)  8.79 us
  transfers between devices with their start and end apart: 9, of which 5 were waited for; matrix products, arithmetic and copies ran while one was open for 20% of the time, Pallas kernels for 0%

commit v1 on v0

v1 whole, which is shorter than its diff:
```python
import functools
import math

import jax
import jax.numpy as jnp
from jax import lax
from jax.experimental import pallas as pl
from jax.experimental.pallas import tpu as pltpu
from jax.sharding import PartitionSpec as P

TILE = 16
MESH = pl.DeviceIdType.MESH
F32, BF16 = jnp.float32, jnp.bfloat16
STEPS = ((-1, 0), (1, 0), (0, -1), (0, 1), (-1, -1), (-1, 1), (1, -1), (1, 1))
PITCH = 64


def halo_bufs(cols, rows, chans):
    return [
        pltpu.VMEM((3, cols, chans), BF16),
        pltpu.VMEM((3, cols, chans), BF16),
        pltpu.VMEM((3, rows, chans), BF16),
        pltpu.VMEM((3, rows, chans), BF16),
        pltpu.VMEM((4, 3, 16, chans), BF16),
        pltpu.SemaphoreType.DMA((8,)),
        pltpu.SemaphoreType.DMA((8,)),
    ]


class Halo:
    def __init__(self, nty, ntx, block, left, right, bufs):
        self.nty, self.ntx = nty, ntx
        self.ty, self.tx = lax.axis_index("ty"), lax.axis_index("tx")
        self.block, self.left, self.right = block, left, right
        self.bufs = bufs

    def there(self, dy, dx):
        ok = None
        for step, at, count in ((dy, self.ty, self.nty), (dx, self.tx, self.ntx)):
            if step:
                one = (at > 0) if step < 0 else (at < count - 1)
                ok = one if ok is None else jnp.logical_and(ok, one)
        return ok

    def greet(self, barrier):
        count = jnp.int32(0)
        for dy, dx in STEPS:
            ok = self.there(dy, dx)

            @pl.when(ok)
            def _(dy=dy, dx=dx):
                pl.semaphore_signal(
                    barrier, inc=1, device_id=(self.ty + dy, self.tx + dx), device_id_type=MESH
                )

            count = count + jnp.where(ok, 1, 0)
        return count

    def copy(self, index):
        dy, dx = STEPS[index]
        top, bottom, left, right, corner, send, recv = self.bufs
        rows = self.block.shape[0]
        src, dst = (
            (self.block.at[0:3], bottom),
            (self.block.at[rows - 3 : rows], top),
            (self.left, right),
            (self.right, left),
            (self.left.at[:, 0:16], corner.at[3]),
            (self.right.at[:, 0:16], corner.at[2]),
            (self.left.at[:, rows - 16 : rows], corner.at[1]),
            (self.right.at[:, rows - 16 : rows], corner.at[0]),
        )[index]
        return pltpu.make_async_remote_copy(
            src_ref=src,
            dst_ref=dst,
            send_sem=send.at[index],
            recv_sem=recv.at[index],
            device_id=(self.ty + dy, self.tx + dx),
            device_id_type=MESH,
        )

    def start(self):
        for index, step in enumerate(STEPS):

            @pl.when(self.there(*step))
            def _(index=index):
                self.copy(index).start()

    def fill(self, work):
        rows, cols, chans = self.block.shape
        halves = chans // 128

        def zero(i, _):
            at = pl.multiple_of(i * PITCH, PITCH)
            work[pl.ds(at, PITCH), :] = jnp.zeros((PITCH, 128), F32)
            return 0

        for h in range(halves):
            lax.fori_loop(h * (rows + 6), h * (rows + 6) + 3, zero, 0)
            lax.fori_loop((h + 1) * (rows + 6) - 3, (h + 1) * (rows + 6), zero, 0)

        def row(i, _):
            for h in range(halves):
                at = pl.multiple_of((h * (rows + 6) + 3 + i) * PITCH, PITCH)
                work[pl.ds(at, 8), :] = jnp.zeros((8, 128), F32)
                work[pl.ds(at + 8, cols), :] = self.block[i, :, h * 128 : h * 128 + 128].astype(F32)
                work[pl.ds(at + 8 + cols, 8), :] = jnp.zeros((8, 128), F32)
            return 0

        lax.fori_loop(0, rows, row, 0)

    def finish(self, work):
        rows, cols, chans = self.block.shape
        halves = chans // 128
        top, bottom, left, right, corner, _, _ = self.bufs
        for index, (dy, dx) in enumerate(STEPS):

            @pl.when(self.there(-dy, -dx))
            def _(index=index):
                self.copy(index).wait_recv()

                for h in range(halves):
                    lanes = slice(h * 128, h * 128 + 128)
                    base = h * (rows + 6)
                    if index < 2:
                        first = 3 + rows if index == 0 else 0
                        src = bottom if index == 0 else top
                        for r in range(3):
                            work[pl.ds((base + first + r) * PITCH + 8, cols), :] = src[r, :, lanes].astype(F32)
                    elif index < 4:
                        first = 8 + cols if index == 2 else 5
                        src = right if index == 2 else left
                        for k in range(3):
                            for g in range(rows // 16):
                                vals = src[k, g * 16 : g * 16 + 16, lanes].astype(F32)
                                for s in range(2):
                                    at = (base + 3 + g * 16 + s * 8) * PITCH + first + k
                                    work[pl.ds(at, 8, stride=PITCH), :] = vals[s * 8 : s * 8 + 8]
                    else:
                        slot = 7 - index
                        low, near = slot < 2, slot % 2 == 0
                        for k in range(3):
                            vals = corner[slot, k, :, lanes].astype(F32)
                            for r in range(3):
                                row = base + (r if low else 3 + rows + r)
                                at = row * PITCH + (5 if near else 8 + cols) + k
                                pick = (13 + r) if low else r
                                work[pl.ds(at, 1), :] = vals[pick : pick + 1]

        for index, step in enumerate(STEPS):

            @pl.when(self.there(*step))
            def _(index=index):
                self.copy(index).wait_send()


def spot(t, rows, cols):
    per = (rows // 4) * (cols // 16)
    h = t // per
    rest = t % per
    r = (rest // (cols // 16)) * 4
    c = (rest % (cols // 16)) * 16
    at = pl.multiple_of((h * (rows + 6) + r) * PITCH + c, 16)
    return h, r, pl.multiple_of(c, 16), at


def conv_block(work, taps, h, at, flip):
    total = [None] * 4
    for b in range(7):
        lines = [work[pl.ds(at + r * PITCH + 5 + b, 16), :] for r in range(10)]
        for a in range(7):
            tap = a * 7 + b
            tap = 48 - tap if flip else tap
            weight = taps[pl.ds(h * 49 + tap, 1), :]
            for o in range(4):
                term = lines[o + a] * weight
                total[o] = term if total[o] is None else total[o] + term
    return total


def pre_kernel(nty, ntx, block, left, right, taps, bias, out, work, *bufs):
    rows, cols, chans = block.shape
    halo = Halo(nty, ntx, block, left, right, bufs)
    barrier = pltpu.get_barrier_semaphore()
    count = halo.greet(barrier)
    pl.semaphore_wait(barrier, count)
    halo.start()
    halo.fill(work)
    halo.finish(work)
    per = (rows // 4) * (cols // 16)
    for half in range(chans // 128):

        def step(t, _, half=half):
            _, r, c, at = spot(t, rows, cols)
            total = conv_block(work, taps, half, at, False)
            for o in range(4):
                out[r + o, pl.ds(c, 16), half * 128 : half * 128 + 128] = total[o] + bias[pl.ds(half, 1), :]
            return 0

        lax.fori_loop(half * per, (half + 1) * per, step, 0)


def post_kernel(
    nty, ntx, size, block, left, right, xblock_pad, cot, taps, sums_in,
    out, sums, dsum, work, dacc, ssend, srecv, gathered, dsend, drecv,
    s_send, s_recv, d_send, d_recv, *bufs,
):
    rows, cols, chans = block.shape
    halves = chans // 128
    halo = Halo(nty, ntx, block, left, right, bufs)
    ty, tx = halo.ty, halo.tx
    bits = [("ty", 1 << k) for k in range(nty.bit_length() - 1)]
    bits += [("tx", 1 << k) for k in range(ntx.bit_length() - 1)]
    nb = len(bits)

    def mine(k):
        axis, bit = bits[k]
        return ((ty if axis == "ty" else tx) // bit) % 2

    def partner(k):
        axis, bit = bits[k]
        step = bit - 2 * bit * mine(k)
        return (ty + step, tx) if axis == "ty" else (ty, tx + step)

    barrier = pltpu.get_barrier_semaphore()
    count = halo.greet(barrier)
    for k in range(nb):
        pl.semaphore_signal(barrier, inc=1, device_id=partner(k), device_id_type=MESH)
    pl.semaphore_wait(barrier, count + nb)
    halo.start()

    lows = [jnp.int32(0)]
    for k in range(nb):
        lows.append(lows[k] + mine(k) * (size >> (k + 1)))

    def by_chunk(length, fn):
        step = min(length, 128)

        def go(i, _):
            fn(pl.multiple_of(i * step, 16), step)
            return 0

        lax.fori_loop(0, length // step, go, 0)

    def rs_copy(k):
        length = size >> (k + 1)
        away = pl.multiple_of(lows[k] + (1 - mine(k)) * length, 16)
        return pltpu.make_async_remote_copy(
            src_ref=ssend.at[pl.ds(away, length)],
            dst_ref=srecv.at[pl.ds(size - 2 * length, length)],
            send_sem=s_send.at[k],
            recv_sem=s_recv.at[k],
            device_id=partner(k),
            device_id_type=MESH,
        )

    def rs_start(k):
        length = size >> (k + 1)
        away = lows[k] + (1 - mine(k)) * length
        source = sums_in if k == 0 else sums

        def cast(i, step):
            at = pl.multiple_of(away + i, 16)
            ssend[pl.ds(at, step), :] = source[pl.ds(at, step), :].astype(BF16)

        by_chunk(length, cast)
        rs_copy(k).start()

    def rs_end(k):
        length = size >> (k + 1)
        source = sums_in if k == 0 else sums
        rs_copy(k).wait()

        def add(i, step):
            at = pl.multiple_of(lows[k + 1] + i, 16)
            got = srecv[pl.ds(pl.multiple_of(size - 2 * length + i, 16), step), :]
            sums[pl.ds(at, step), :] = source[pl.ds(at, step), :] + got.astype(F32)

        by_chunk(length, add)

    def ag_copy(k):
        length = size >> (k + 1)
        at = pl.multiple_of(lows[k + 1], 16)
        return pltpu.make_async_remote_copy(
            src_ref=gathered.at[pl.ds(at, length)],
            dst_ref=gathered.at[pl.ds(at, length)],
            send_sem=s_send.at[nb + k],
            recv_sem=s_recv.at[nb + k],
            device_id=partner(k),
            device_id_type=MESH,
        )

    def ag_start(k):
        if k == nb - 1:
            length = size >> nb

            def cast(i, step):
                at = pl.multiple_of(lows[nb] + i, 16)
                gathered[pl.ds(at, step), :] = sums[pl.ds(at, step), :].astype(BF16)

            by_chunk(length, cast)
        ag_copy(k).start()

    def d_copy(k):
        return pltpu.make_async_remote_copy(
            src_ref=dsend.at[k],
            dst_ref=drecv.at[k],
            send_sem=d_send.at[k],
            recv_sem=d_recv.at[k],
            device_id=partner(k),
            device_id_type=MESH,
        )

    events = []
    for k in range(nb):
        events.append((functools.partial(rs_start, k), functools.partial(rs_end, k)))
    for k in reversed(range(nb)):
        events.append((functools.partial(ag_start, k), ag_copy(k).wait))
    d_events = [(d_copy(k).start, functools.partial(lambda k: d_end(k), k)) for k in range(nb)]

    def d_end(k):
        d_copy(k).wait()
        new = dsend[k] + drecv[k]
        if k + 1 < nb:
            dsend[k + 1] = new
        else:
            dsum[...] = new

    events[0][0]()
    at_event = [0, 0]

    def advance(upto, which, line):
        while at_event[which] < upto:
            e = at_event[which]
            line[e][1]()
            if e + 1 < len(line):
                line[e + 1][0]()
            at_event[which] += 1

    halo.fill(work)

    dacc[...] = jnp.zeros_like(dacc)
    blocks = halves * (rows // 4) * (cols // 16)

    def grad_step(t, _):
        h, r, c, at = spot(t, rows, cols)
        mid = pl.multiple_of(at + 3 * PITCH + 8, 8)
        gs = [work[pl.ds(mid + o * PITCH, 16), :] for o in range(4)]
        for b in range(7):
            lines = [xblock_pad[pl.ds(at + q * PITCH + 5 + b, 16), :] for q in range(10)]
            for a in range(7):
                term = lines[a] * gs[0]
                for o in range(1, 4):
                    term = term + lines[o + a] * gs[o]
                slot = pl.multiple_of((h * 49 + a * 7 + b) * 8, 8)
                dacc[pl.ds(slot, 8), :] = dacc[pl.ds(slot, 8), :] + (term[:8] + term[8:])
        return 0

    def out_step(half, t, _):
        _, r, c, at = spot(t, rows, cols)
        total = conv_block(work, taps, half, at, True)
        for o in range(4):
            lanes = slice(half * 128, half * 128 + 128)
            res = total[o] + cot[r + o, pl.ds(c, 16), lanes].astype(F32)
            out[r + o, pl.ds(c, 16), lanes] = res.astype(BF16)
        return 0

    pieces = 4
    each = blocks // pieces
    for p in range(pieces):
        lax.fori_loop(p * each, (p + 1) * each, grad_step, 0)
        advance(len(events) * (p + 1) // (2 * pieces), 0, events)

    def fold(i, _):
        at = pl.multiple_of(i * 8, 8)
        dsend[0, pl.ds(i, 1), :] = jnp.sum(dacc[pl.ds(at, 8), :], axis=0, keepdims=True)
        return 0

    dsend[0, 96:104, :] = jnp.zeros((8, 128), F32)
    lax.fori_loop(0, halves * 49, fold, 0)
    d_events[0][0]()
    halo.finish(work)
    for p in range(pieces):
        lax.fori_loop(
            p * each, (p + 1) * each, functools.partial(out_step, p * halves // pieces), 0
        )
        advance(len(events) * (pieces + p + 1) // (2 * pieces), 0, events)
        advance(nb * (p + 1) // pieces, 1, d_events)

    def widen(i, step):
        sums[pl.ds(i, step), :] = gathered[pl.ds(i, step), :].astype(F32)

    by_chunk(size, widen)


def strips(block):
    cols = block.shape[1]
    return (
        jnp.transpose(block[:, :3], (1, 0, 2)),
        jnp.transpose(block[:, cols - 3 :], (1, 0, 2)),
    )


def branch_back(pre, masked, ln_gain, ln_bias, w_expand, b_expand, w_reduce, layer_scale):
    center = pre - jnp.mean(pre, axis=-1, keepdims=True)
    rstd = lax.rsqrt(jnp.mean(center * center, axis=-1, keepdims=True) + 1e-06)
    nhat = center * rstd
    normed = (nhat * ln_gain + ln_bias).astype(BF16)
    zvals = jnp.dot(normed, w_expand, preferred_element_type=F32) + b_expand
    cdf = 0.5 * (1.0 + jax.scipy.special.erf(zvals * 0.7071067811865476))
    hidden = (zvals * cdf).astype(BF16)
    go_vals = (layer_scale * masked.astype(F32)).astype(BF16)
    dhid = jnp.dot(go_vals, w_reduce.T, preferred_element_type=F32)
    slope = cdf + zvals * jnp.exp(-0.5 * zvals * zvals) * 0.3989422804014327
    dzvals = (dhid * slope).astype(BF16)
    dnorm = jnp.dot(dzvals, w_expand.T, preferred_element_type=F32) * ln_gain
    grad = rstd * (
        dnorm
        - jnp.mean(dnorm, axis=-1, keepdims=True)
        - nhat * jnp.mean(dnorm * nhat, axis=-1, keepdims=True)
    )
    return (grad.astype(BF16), hidden, normed, go_vals, dzvals)


def body(
    nty,
    ntx,
    block_input,
    cotangent,
    tissue,
    dw_weight,
    dw_bias,
    ln_gain,
    ln_bias,
    w_expand,
    b_expand,
    w_reduce,
    layer_scale,
):
    rows, cols, chans = block_input.shape
    hid = w_expand.shape[1]
    halves = chans // 128
    padded = halves * (rows + 6) * PITCH
    taps = jnp.transpose(dw_weight.reshape(49, halves, 128), (1, 0, 2)).reshape(halves * 49, 128)
    vmem = pl.BlockSpec(memory_space=pltpu.VMEM)
    flops = 49 * 2 * rows * cols * chans
    pre, xpad = pl.pallas_call(
        functools.partial(pre_kernel, nty, ntx),
        out_shape=(
            jax.ShapeDtypeStruct((rows, cols, chans), F32),
            jax.ShapeDtypeStruct((padded, 128), F32),
        ),
        in_specs=[vmem] * 5,
        out_specs=(vmem, vmem),
        scratch_shapes=halo_bufs(cols, rows, chans),
        compiler_params=pltpu.CompilerParams(
            collective_id=0, has_side_effects=True, vmem_limit_bytes=40 << 20
        ),
        cost_estimate=pl.CostEstimate(flops=flops, bytes_accessed=16 << 20, transcendentals=0),
        name="pre",
    )(block_input, *strips(block_input), taps, dw_bias.reshape(halves, 128))

    mask = jnp.repeat(jnp.repeat(tissue, TILE, axis=0), TILE, axis=1)
    masked = (cotangent.astype(F32) * mask[:, :, None].astype(F32)).astype(BF16)
    params = (ln_gain, ln_bias, w_expand, b_expand, w_reduce, layer_scale)
    grad, hidden, normed, go_vals, dzvals = branch_back(
        pre.reshape(-1, chans), masked.reshape(-1, chans), *params
    )
    grad_core = grad.reshape(rows, cols, chans)
    local_reduce = jnp.dot(hidden.T, go_vals, preferred_element_type=F32)
    local_expand = jnp.dot(normed.T, dzvals, preferred_element_type=F32)

    wide = hid // 128
    sums_in = jnp.concatenate(
        [local_expand[:, k * 128 : (k + 1) * 128] for k in range(wide)]
        + [local_reduce[:, k * 128 : (k + 1) * 128] for k in range(halves)]
    )
    used = sums_in.shape[0]
    unit = nty * ntx * 16
    size = -(-used // unit) * unit
    if size != used:
        sums_in = jnp.pad(sums_in, ((0, size - used), (0, 0)))
    nb = (nty * ntx).bit_length() - 1
    out, sums, dsum = pl.pallas_call(
        functools.partial(post_kernel, nty, ntx, size),
        out_shape=(
            jax.ShapeDtypeStruct((rows, cols, chans), BF16),
            jax.ShapeDtypeStruct((size, 128), F32),
            jax.ShapeDtypeStruct((104, 128), F32),
        ),
        in_specs=[vmem] * 7,
        out_specs=(vmem,) * 3,
        scratch_shapes=[
            pltpu.VMEM((padded, 128), F32),
            pltpu.VMEM((halves * 49 * 8, 128), F32),
            pltpu.VMEM((size, 128), BF16),
            pltpu.VMEM((size, 128), BF16),
            pltpu.VMEM((size, 128), BF16),
            pltpu.VMEM((nb, 104, 128), F32),
            pltpu.VMEM((nb, 104, 128), F32),
            pltpu.SemaphoreType.DMA((2 * nb,)),
            pltpu.SemaphoreType.DMA((2 * nb,)),
            pltpu.SemaphoreType.DMA((nb,)),
            pltpu.SemaphoreType.DMA((nb,)),
        ]
        + halo_bufs(cols, rows, chans),
        compiler_params=pltpu.CompilerParams(
            collective_id=1, has_side_effects=True, vmem_limit_bytes=50 << 20
        ),
        cost_estimate=pl.CostEstimate(flops=2 * flops, bytes_accessed=24 << 20, transcendentals=0),
        name="post",
    )(grad_core, *strips(grad_core), xpad, cotangent, taps, sums_in)

    factor = 1.0 / math.sqrt(rows * nty * cols * ntx)
    total_expand = jnp.concatenate([sums[k * chans : (k + 1) * chans] for k in range(wide)], axis=1)
    base = wide * chans
    total_reduce = jnp.concatenate(
        [sums[base + k * hid : base + (k + 1) * hid] for k in range(halves)], axis=1
    )
    total_dw = jnp.concatenate([dsum[k * 49 : (k + 1) * 49] for k in range(halves)], axis=1)
    return (out, total_dw * factor, total_expand * factor, total_reduce * factor)


def solution(mesh):
    placed = (P("ty", "tx", None), P("ty", "tx", None), P("ty", "tx")) + (P(),) * 8
    return jax.shard_map(
        functools.partial(body, mesh.shape["ty"], mesh.shape["tx"]),
        mesh=mesh,
        in_specs=placed,
        out_specs=(P("ty", "tx", None), P(), P(), P()),
        check_vma=False,
    )
```

time: 357 us -> 141 us (0.39)
  other arithmetic: 143 us -> 16.8 us
  waiting for transfers between devices: 107 us -> 0 us
  Pallas kernels: 0 us -> 87.6 us
  blocking collectives: 41.6 us -> 0 us
  starting transfers between devices: 18.4 us -> 0 us
  between operations: 14.7 us -> 1.06 us
  local copies, waits for them, and re-layouts: 7.49 us -> 17.9 us
  matrix products: 23.2 us -> 17.4 us
    psum x1 -> x0, waiting for transfers between devices: 95.4 us -> none  [body(): lax.psum((local_expand, local_reduce, local_dw), ('ty', 'tx'))]
    pallas_call x0 -> x2, Pallas kernels: none -> 87.6 us  [the longest x1 60.4 us: body(): pl.pallas_call(functools.partial(post_kernel, nty, ntx, size), out_shape=...]
    reduce_sum x1, other arithmetic: 61.1 us -> 2.39 us  [branch_back(): center = pre - jnp.mean(pre, axis=-1, keepdims=True)]
    psum x1 -> x0, blocking collectives: 41.6 us -> none  [body(): lax.psum((local_expand, local_reduce, local_dw), ('ty', 'tx'))]
    convert_element_type x6 -> x5, other arithmetic: 43.1 us -> 8.8 us  [the longest x1 3.1 us: branch_back(): normed = (nhat * ln_gain + ln_bias).astype(BF16)]
    reduce_sum x6 -> x0, other arithmetic: 28.4 us -> none  [filter_grad(): taps.append(jnp.sum(window * gradf, axis=(0, 1)))]
    ppermute x8 -> x0, starting transfers between devices: 18.3 us -> none  [the longest x4 13.2 us: with_halo(): lax.ppermute(lax.slice_in_dim(block, block.shape[dim] - width, None, axis...]
    ppermute x8 -> x0, waiting for transfers between devices: 12 us -> none  [the longest x4 8.79 us: with_halo(): lax.ppermute(lax.slice_in_dim(block, 0, width, axis=dim), axis, backward)]
  transfers between devices with their start and end apart: 9 -> 0, of which waited for: 5 -> 0; matrix products, arithmetic and copies ran while one was open for 20% -> 0% of each run, Pallas kernels for 0% -> 0%
where the time goes in v1:
time: 141 us
  Pallas kernels  87.6 us (62%)
  local copies, waits for them, and re-layouts  17.9 us (13%)
  matrix products  17.4 us (12%)
  other arithmetic  16.8 us (12%)
    pallas_call x1, Pallas kernels, body(): pl.pallas_call(functools.partial(post_kernel, nty, ntx, size), out_shape=...  60.4 us
    pallas_call x1, Pallas kernels, body(): pl.pallas_call(functools.partial(pre_kernel, nty, ntx), out_shape=(jax.Sh...  27.3 us
    unnamed x43, local copies, waits for them, and re-layouts  13 us
    dot_general x1, matrix products, branch_back(): dhid = jnp.dot(go_vals, w_reduce.T, preferred_element_type=F32)  6.77 us
    dot_general x1, matrix products, body(): local_reduce = jnp.dot(hidden.T, go_vals, preferred_element_type=F32)  4.57 us
    convert_element_type x1, other arithmetic, branch_back(): normed = (nhat * ln_gain + ln_bias).astype(BF16)  3.1 us

profile of v1, /device:TPU:0, one launch (start us, length us, event | category | flops | bytes accessed | tf_op | source)
XLA Modules:
  0.0 140.8 jit_solution(6478828423908674879)
XLA Ops:
  0.7 0.7 convert_element_type.44
  1.7 0.9 reshape.80
  2.6 1.1 fusion.13
  3.8 2.0 %multiply_convert_fusion.3 = bf16[64,48,256]{2,1,0:T(8,128)(2,1)S(1)} fusion(bf16[64,48,256]{2,1,0:T(8,128)(2,1)} %cot.1, f32[64,48]{1,0:T(8,128)S(1)} %copy.23), kind=kLoop, calls=%fused_computation.19 | loop fusion | flops 2359296 | bytes 3158016 | tf_op jit(solution)/shard_map/convert_element_type | solution.py:464
  5.9 0.4 fusion.8
  6.3 27.3 %pre.1 = (f32[64,48,256]{2,1,0:T(8,128)S(1)}, f32[8960,128]{1,0:T(8,128)S(1)}) custom-call(bf16[64,48,256]{2,1,0:T(8,128)(2,1)S(1)} %copy-done.4, bf16[3,64,256]{2,1,0:T(8,128)(2,1)S(1)} %get-tuple-element.26.left, bf16[3,64,256]{2,1,0:T(8,128)(2,1)S(1)} %get-tuple-element.25.right, f32[98,128]{1,0:T(8,128)S(1)} %reshape.81.taps, f32[2,128]{1,0:T(2,128)S(1)} %bitcast.44), custom_call_target="tpu_custom_call" | custom-call | flops 77070336 | bytes 16777216 | tf_op jit(solution)/shard_map/pre/pallas_call | solution.py:447
  33.6 1.7 %copy-done.1 = f32[64,48,256]{2,1,0:T(8,128)} copy-done((f32[64,48,256]{2,1,0:T(8,128)}, f32[64,48,256]{2,1,0:T(8,128)S(1)}, u32[]{:S(2)}) %copy-start.1) | copy-done | bytes 3145752
  35.3 2.1 %copy-done.3 = f32[8960,128]{1,0:T(8,128)} copy-done((f32[8960,128]{1,0:T(8,128)}, f32[8960,128]{1,0:T(8,128)S(1)}, u32[]{:S(2)}) %copy-start.3) | copy-done | bytes 4587544
  37.4 2.4 %reduce_sum.36 = f32[64,48]{1,0:T(8,128)S(1)} reduce(f32[64,48,256]{2,1,0:T(8,128)} %copy-done.1, f32[]{:T(128)} %constant.9.clone.1), dimensions={2}, to_apply=%region_0.0 | reduce | flops 783360 | bytes 3158020 | tf_op jit(solution)/shard_map/reduce_sum | solution.py:405
  39.9 2.8 %multiply_reduce_fusion.1 = f32[64,48]{1,0:T(8,128)S(1)} fusion(f32[64,48,256]{2,1,0:T(8,128)} %copy-done.1, f32[64,48]{1,0:T(8,128)S(1)} %broadcast_multiply_fusion.1), kind=kLoop, calls=%fused_computation.20 | loop fusion | flops 2356224 | bytes 3170304 | tf_op jit(solution)/shard_map/reduce_sum | solution.py:406
  42.8 3.1 %add_convert_fusion = bf16[3072,256]{1,0:T(8,128)(2,1)S(1)} fusion(f32[64,48,256]{2,1,0:T(8,128)} %copy-done.1, f32[256]{0:T(256)S(1)} %copy-done.8, f32[256]{0:T(256)S(1)} %copy-done.9, f32[3072]{0:T(1024)S(1)} %div.16, f32[3072]{0:T(1024)S(1)} %rsqrt.12), kind=kLoop, calls=%fused_computation.18 | loop fusion | flops 3932160 | bytes 4745216 | tf_op jit(solution)/shard_map/convert_element_type | solution.py:408
  45.9 1.8 %fusion.15 = f32[3072,1024]{1,0:T(8,128)S(1)} fusion(bf16[3072,256]{1,0:T(8,128)(2,1)S(1)} %add_convert_fusion, bf16[256,1024]{1,0:T(8,128)(2,1)S(1)} %copy-done), kind=kOutput, calls=%fused_computation.56 | convolution fusion | flops 1610612736 | bytes 14680064 | tf_op jit(solution)/shard_map/dot_general | solution.py:409
  47.7 4.6 %fusion.6 = f32[1024,256]{1,0:T(8,128)S(1)} fusion(bf16[3072,256]{1,0:T(8,128)(2,1)S(1)} %fusion.8, f32[3072,1024]{1,0:T(8,128)S(1)} %fusion.15, f32[1024]{0:T(1024)S(1)} %copy-done.11), kind=kOutput, calls=%fused_computation.9 | convolution fusion | flops 1629487104 | bytes 15208448 | tf_op jit(solution)/shard_map/dot_general | solution.py:470
  52.3 6.8 %fusion.5 = bf16[3072,1024]{1,0:T(8,128)(2,1)S(1)} fusion(f32[3072,1024]{1,0:T(8,128)S(1)} %fusion.15, bf16[3072,256]{1,0:T(8,128)(2,1)S(1)} %fusion.8, bf16[1024,256]{1,0:T(8,128)(2,1)S(1)} %copy-done.10, f32[1024]{0:T(1024)S(1)} %copy-done.11), kind=kOutput, calls=%fused_computation.6 | convolution fusion | flops 1645215744 | bytes 20975616 | tf_op jit(solution)/shard_map/dot_general | solution.py:413
  59.1 1.8 %fusion.16 = f32[256,1024]{1,0:T(8,128)S(1)} fusion(bf16[3072,256]{1,0:T(8,128)(2,1)S(1)} %add_convert_fusion, bf16[3072,1024]{1,0:T(8,128)(2,1)S(1)} %fusion.5), kind=kOutput, calls=%fused_computation.57 | convolution fusion | flops 1610612736 | bytes 8912896 | tf_op jit(solution)/shard_map/dot_general | solution.py:471
  61.0 2.5 %fusion.10 = (f32[3072]{0:T(1024)S(1)}, f32[3072]{0:T(1024)S(1)}, f32[3072,256]{1,0:T(8,128)S(1)}) fusion(f32[3072]{0:T(1024)S(1)} %rsqrt.12, f32[3072]{0:T(1024)S(1)} %div.16, f32[64,48,256]{2,1,0:T(8,128)S(1)} %copy-done.2, f32[256]{0:T(256)S(1)} %copy-done.9, bf16[3072,1024]{1,0:T(8,128)(2,1)S(1)} %fusion.5, bf16[256,1024]{1,0:T(8,128)(2,1)S(1)} %copy-done), kind=kOutput, calls=%fused_computation.51 | convolution fusion | flops 1615325184 | bytes 13157376 | tf_op jit(solution)/shard_map/dot_general | solution.py:416
  63.5 2.5 %multiply_convert_fusion.2 = bf16[3072,256]{1,0:T(8,128)(2,1)S(1)} fusion(f32[3072,256]{1,0:T(8,128)S(1)} %get-tuple-element.24, f32[64,48,256]{2,1,0:T(8,128)S(1)} %copy-done.2, f32[3072]{0:T(1024)S(1)} %broadcast_multiply_fusion.2, f32[3072]{0:T(1024)S(1)} %broadcast_multiply_fusion.3, f32[3072]{0:T(1024)S(1)} %div.16, f32[3072]{0:T(1024)S(1)} %rsqrt.12), kind=kLoop, calls=%fused_computation.16 | loop fusion | flops 5505024 | bytes 7913472 | tf_op jit(solution)/shard_map/convert_element_type | solution.py:422
  66.4 1.4 copy-done.6
  67.8 60.4 %post.1 = (bf16[64,48,256]{2,1,0:T(8,128)(2,1)S(1)}, f32[4096,128]{1,0:T(8,128)}, f32[104,128]{1,0:T(8,128)S(1)}) custom-call(bf16[64,48,256]{2,1,0:T(8,128)(2,1)S(1)} %bitcast.41, bf16[3,64,256]{2,1,0:T(8,128)(2,1)S(1)} %bitcast.43, bf16[3,64,256]{2,1,0:T(8,128)(2,1)S(1)} %bitcast.42, f32[8960,128]{1,0:T(8,128)} %copy-done.3, bf16[64,48,256]{2,1,0:T(8,128)(2,1)} %cot.1, ...), custom_call_target="tpu_custom_call" | custom-call | flops 154140672 | bytes 25165824 | tf_op jit(solution)/shard_map/post/pallas_call | solution.py:484
  128.2 0.6 maximum_multiply_fusion.1
  128.8 0.9 slice_dynamic-update-slice_fusion.17
  129.7 0.9 slice_dynamic-update-slice_fusion.16
  130.6 0.9 slice_dynamic-update-slice_fusion.15
  131.6 0.9 slice_dynamic-update-slice_fusion.14
  132.5 0.9 slice_dynamic-update-slice_fusion.13
  133.4 0.9 slice_dynamic-update-slice_fusion.12
  134.3 0.9 slice_dynamic-update-slice_fusion.11
  135.2 0.9 slice_dynamic-update-slice_fusion.10
  136.2 1.3 fusion.11
  137.4 1.1 maximum_multiply_fusion
  138.5 1.1 broadcast_multiply_fusion
  139.6 1.1 copy.55
  (49 shorter events, 1.0 us)
Async XLA Ops:
  0.6 45.2 %copy-start = (bf16[256,1024]{1,0:T(8,128)(2,1)S(1)}, bf16[256,1024]{1,0:T(8,128)(2,1)}, u32[]{:S(2)}) copy-start(bf16[256,1024]{1,0:T(8,128)(2,1)} %param.18) | copy-start | bytes 1572868
  0.6 5.2 %copy-start.7 = (f32[256]{0:T(256)S(1)}, f32[256]{0:T(256)}, u32[]{:S(2)}) copy-start(f32[256]{0:T(256)} %param.21) | copy-start | bytes 3076
  3.8 2.5 %copy-start.4 = (bf16[64,48,256]{2,1,0:T(8,128)(2,1)S(1)}, bf16[64,48,256]{2,1,0:T(8,128)(2,1)}, u32[]{:S(2)}) copy-start(bf16[64,48,256]{2,1,0:T(8,128)(2,1)} %block.1) | copy-start | bytes 4718596
  3.8 2.5 %copy-start.5 = (f32[256]{0:T(256)S(1)}, f32[256]{0:T(256)}, u32[]{:S(2)}) copy-start(f32[256]{0:T(256)} %param.15) | copy-start | bytes 3076
  33.6 1.7 %copy-start.1 = (f32[64,48,256]{2,1,0:T(8,128)}, f32[64,48,256]{2,1,0:T(8,128)S(1)}, u32[]{:S(2)}) copy-start(f32[64,48,256]{2,1,0:T(8,128)S(1)} %get-tuple-element.9) | copy-start | bytes 9437188
  35.3 2.1 %copy-start.3 = (f32[8960,128]{1,0:T(8,128)}, f32[8960,128]{1,0:T(8,128)S(1)}, u32[]{:S(2)}) copy-start(f32[8960,128]{1,0:T(8,128)S(1)} %get-tuple-element.10.xblock_pad) | copy-start | bytes 13762564
  37.4 5.4 %copy-start.8 = (f32[256]{0:T(256)S(1)}, f32[256]{0:T(256)}, u32[]{:S(2)}) copy-start(f32[256]{0:T(256)} %param.17) | copy-start | bytes 3076
  37.4 5.4 %copy-start.9 = (f32[256]{0:T(256)S(1)}, f32[256]{0:T(256)}, u32[]{:S(2)}) copy-start(f32[256]{0:T(256)} %param.16) | copy-start | bytes 3076
  45.9 1.8 %copy-start.11 = (f32[1024]{0:T(1024)S(1)}, f32[1024]{0:T(1024)}, u32[]{:S(2)}) copy-start(f32[1024]{0:T(1024)} %param.19) | copy-start | bytes 12292
  47.7 4.6 %copy-start.10 = (bf16[1024,256]{1,0:T(8,128)(2,1)S(1)}, bf16[1024,256]{1,0:T(8,128)(2,1)}, u32[]{:S(2)}) copy-start(bf16[1024,256]{1,0:T(8,128)(2,1)} %param.20) | copy-start | bytes 1572868
  59.1 1.9 %copy-start.2 = (f32[64,48,256]{2,1,0:T(8,128)S(1)}, f32[64,48,256]{2,1,0:T(8,128)}, u32[]{:S(2)}) copy-start(f32[64,48,256]{2,1,0:T(8,128)} %copy-done.1) | copy-start | bytes 9437188
  66.4 1.4 copy-start.6

commit v2 on v1

--- a/solution.py
+++ b/solution.py
@@ -186,23 +186,41 @@
     pl.semaphore_wait(barrier, count)
     halo.start()
     halo.fill(work)
+
+    def block_at(half, r, c):
+        at = pl.multiple_of((half * (rows + 6) + r) * PITCH + c, 16)
+        total = conv_block(work, taps, half, at, False)
+        for o in range(4):
+            lanes = slice(half * 128, half * 128 + 128)
+            out[r + o, pl.ds(c, 16), lanes] = total[o] + bias[pl.ds(half, 1), :]
+
+    inner = cols // 16 - 2
+    for half in range(chans // 128):
+
+        def inside(t, _, half=half):
+            block_at(half, (1 + t // inner) * 4, pl.multiple_of((1 + t % inner) * 16, 16))
+            return 0
+
+        lax.fori_loop(0, (rows // 4 - 2) * inner, inside, 0)
     halo.finish(work)
-    per = (rows // 4) * (cols // 16)
     for half in range(chans // 128):
 
-        def step(t, _, half=half):
-            _, r, c, at = spot(t, rows, cols)
-            total = conv_block(work, taps, half, at, False)
-            for o in range(4):
-                out[r + o, pl.ds(c, 16), half * 128 : half * 128 + 128] = total[o] + bias[pl.ds(half, 1), :]
+        def edge(t, _, half=half):
+            block_at(half, (1 + t // 2) * 4, pl.multiple_of((t % 2) * (cols - 16), 16))
             return 0
 
-        lax.fori_loop(half * per, (half + 1) * per, step, 0)
+        def ends(t, _, half=half):
+            wide = cols // 16
+            block_at(half, (t // wide) * (rows - 4), pl.multiple_of((t % wide) * 16, 16))
+            return 0
+
+        lax.fori_loop(0, (rows // 4 - 2) * 2, edge, 0)
+        lax.fori_loop(0, 2 * (cols // 16), ends, 0)
 
 
 def post_kernel(
-    nty, ntx, size, block, left, right, xblock_pad, cot, taps, sums_in,
-    out, sums, dsum, work, dacc, ssend, srecv, gathered, dsend, drecv,
+    nty, ntx, size, wide, factor, block, left, right, xblock_pad, cot, taps, sums_in,
+    out, dw, expand, reduce, sums, dsum, work, dacc, ssend, srecv, gathered, dsend, drecv,
     s_send, s_recv, d_send, d_recv, *bufs,
 ):
     rows, cols, chans = block.shape
@@ -337,8 +355,10 @@
                 line[e + 1][0]()
             at_event[which] += 1
 
+    def due(count, done, over):
+        return min(count, -(-count * done // over))
+
     halo.fill(work)
-
     dacc[...] = jnp.zeros_like(dacc)
     blocks = halves * (rows // 4) * (cols // 16)
 
@@ -365,11 +385,11 @@
             out[r + o, pl.ds(c, 16), lanes] = res.astype(BF16)
         return 0
 
-    pieces = 4
+    pieces = 6
     each = blocks // pieces
     for p in range(pieces):
         lax.fori_loop(p * each, (p + 1) * each, grad_step, 0)
-        advance(len(events) * (p + 1) // (2 * pieces), 0, events)
+        advance(due(len(events), p + 1, 2 * pieces - 1), 0, events)
 
     def fold(i, _):
         at = pl.multiple_of(i * 8, 8)
@@ -384,13 +404,16 @@
         lax.fori_loop(
             p * each, (p + 1) * each, functools.partial(out_step, p * halves // pieces), 0
         )
-        advance(len(events) * (pieces + p + 1) // (2 * pieces), 0, events)
-        advance(nb * (p + 1) // pieces, 1, d_events)
-
-    def widen(i, step):
-        sums[pl.ds(i, step), :] = gathered[pl.ds(i, step), :].astype(F32)
-
-    by_chunk(size, widen)
+        advance(due(len(events), pieces + p + 1, 2 * pieces - 1), 0, events)
+        advance(due(nb, p + 1, pieces - 1), 1, d_events)
+
+    for k in range(wide):
+        expand[:, k * 128 : (k + 1) * 128] = gathered[k * chans : (k + 1) * chans, :].astype(F32) * factor
+        at = (wide + k) * chans
+        part = gathered[at : at + chans, :].astype(F32) * factor
+        reduce[k * 128 : (k + 1) * 128, :] = jnp.transpose(part)
+    for h in range(halves):
+        dw[:, h * 128 : (h + 1) * 128] = dsum[h * 49 : (h + 1) * 49, :] * factor
 
 
 def strips(block):
@@ -401,25 +424,63 @@
     )
 
 
-def branch_back(pre, masked, ln_gain, ln_bias, w_expand, b_expand, w_reduce, layer_scale):
-    center = pre - jnp.mean(pre, axis=-1, keepdims=True)
+def contract(left, right, ldim, rdim):
+    return lax.dot_general(
+        left, right, (((ldim,), (rdim,)), ((), ())), preferred_element_type=F32
+    )
+
+
+def mid_kernel(pre, cot, tissue, gain, shift, w_expand, b_expand, w_reduce, scale, grad, sums):
+    rows, cols, chans = pre.shape
+    hid = w_expand.shape[1]
+    pixels = rows * cols
+    turn = pl.program_id(0)
+
+    @pl.when(turn == 0)
+    def _():
+        sums[...] = jnp.zeros_like(sums)
+
+    masked = jnp.concatenate(
+        [
+            cot[:, k * TILE : (k + 1) * TILE, :].astype(F32) * tissue[turn, k].astype(F32)
+            for k in range(cols // TILE)
+        ],
+        axis=1,
+    ).reshape(pixels, chans)
+    go_vals = (scale[...] * masked).astype(BF16)
+    vals = pre[...].reshape(pixels, chans)
+    center = vals - jnp.mean(vals, axis=-1, keepdims=True)
     rstd = lax.rsqrt(jnp.mean(center * center, axis=-1, keepdims=True) + 1e-06)
     nhat = center * rstd
-    normed = (nhat * ln_gain + ln_bias).astype(BF16)
-    zvals = jnp.dot(normed, w_expand, preferred_element_type=F32) + b_expand
-    cdf = 0.5 * (1.0 + jax.scipy.special.erf(zvals * 0.7071067811865476))
-    hidden = (zvals * cdf).astype(BF16)
-    go_vals = (layer_scale * masked.astype(F32)).astype(BF16)
-    dhid = jnp.dot(go_vals, w_reduce.T, preferred_element_type=F32)
-    slope = cdf + zvals * jnp.exp(-0.5 * zvals * zvals) * 0.3989422804014327
-    dzvals = (dhid * slope).astype(BF16)
-    dnorm = jnp.dot(dzvals, w_expand.T, preferred_element_type=F32) * ln_gain
-    grad = rstd * (
+    normed = (nhat * gain[...] + shift[...]).astype(BF16)
+    go_t = jnp.transpose(go_vals)
+    normed_t = jnp.transpose(normed)
+    part = 256
+    dnorm = None
+    for k in range(hid // part):
+        span = slice(k * part, (k + 1) * part)
+        zvals = contract(normed, w_expand[:, span], 1, 0) + b_expand[:, span]
+        cdf = 0.5 * (1.0 + lax.erf(zvals * 0.7071067811865476))
+        hidden = (zvals * cdf).astype(BF16)
+        slope = cdf + zvals * jnp.exp(-0.5 * zvals * zvals) * 0.3989422804014327
+        dzvals = (contract(go_vals, w_reduce[span, :], 1, 1) * slope).astype(BF16)
+        term = contract(dzvals, w_expand[:, span], 1, 1)
+        dnorm = term if dnorm is None else dnorm + term
+        to_expand = contract(normed_t, dzvals, 1, 0)
+        to_reduce = contract(go_t, hidden, 1, 0)
+        for j in range(part // 128):
+            lanes = slice(j * 128, (j + 1) * 128)
+            at = (k * (part // 128) + j) * chans
+            sums[at : at + chans, :] += to_expand[:, lanes]
+            at += hid // 128 * chans
+            sums[at : at + chans, :] += to_reduce[:, lanes]
+    dnorm = dnorm * gain[...]
+    result = rstd * (
         dnorm
         - jnp.mean(dnorm, axis=-1, keepdims=True)
         - nhat * jnp.mean(dnorm * nhat, axis=-1, keepdims=True)
     )
-    return (grad.astype(BF16), hidden, normed, go_vals, dzvals)
+    grad[...] = result.astype(BF16).reshape(rows, cols, chans)
 
 
 def body(
@@ -460,37 +521,53 @@
         name="pre",
     )(block_input, *strips(block_input), taps, dw_bias.reshape(halves, 128))
 
-    mask = jnp.repeat(jnp.repeat(tissue, TILE, axis=0), TILE, axis=1)
-    masked = (cotangent.astype(F32) * mask[:, :, None].astype(F32)).astype(BF16)
-    params = (ln_gain, ln_bias, w_expand, b_expand, w_reduce, layer_scale)
-    grad, hidden, normed, go_vals, dzvals = branch_back(
-        pre.reshape(-1, chans), masked.reshape(-1, chans), *params
-    )
-    grad_core = grad.reshape(rows, cols, chans)
-    local_reduce = jnp.dot(hidden.T, go_vals, preferred_element_type=F32)
-    local_expand = jnp.dot(normed.T, dzvals, preferred_element_type=F32)
-
     wide = hid // 128
-    sums_in = jnp.concatenate(
-        [local_expand[:, k * 128 : (k + 1) * 128] for k in range(wide)]
-        + [local_reduce[:, k * 128 : (k + 1) * 128] for k in range(halves)]
-    )
-    used = sums_in.shape[0]
     unit = nty * ntx * 16
-    size = -(-used // unit) * unit
-    if size != used:
-        sums_in = jnp.pad(sums_in, ((0, size - used), (0, 0)))
-    nb = (nty * ntx).bit_length() - 1
-    out, sums, dsum = pl.pallas_call(
-        functools.partial(post_kernel, nty, ntx, size),
+    size = -(-2 * wide * chans // unit) * unit
+    one = lambda array: pl.BlockSpec(array.shape, lambda i: (0,) * array.ndim)
+    per_tile = pl.BlockSpec((TILE, cols, chans), lambda i: (i, 0, 0))
+    whole = [
+        ln_gain.reshape(1, chans),
+        ln_bias.reshape(1, chans),
+        w_expand,
+        b_expand.reshape(1, hid),
+        w_reduce,
+        layer_scale.reshape(1, chans),
+    ]
+    grad_core, sums_in = pl.pallas_call(
+        mid_kernel,
+        grid=(rows // TILE,),
         out_shape=(
             jax.ShapeDtypeStruct((rows, cols, chans), BF16),
             jax.ShapeDtypeStruct((size, 128), F32),
-            jax.ShapeDtypeStruct((104, 128), F32),
+        ),
+        in_specs=[per_tile, per_tile, pl.BlockSpec(memory_space=pltpu.SMEM)]
+        + [one(array) for array in whole],
+        out_specs=(per_tile, pl.BlockSpec((size, 128), lambda i: (0, 0))),
+        compiler_params=pltpu.CompilerParams(vmem_limit_bytes=44 << 20),
+        cost_estimate=pl.CostEstimate(
+            flops=10 * rows * cols * chans * hid,
+            bytes_accessed=12 << 20,
+            transcendentals=2 * rows * cols * hid,
+        ),
+        name="mid",
+    )(pre, cotangent, tissue, *whole)
+
+    factor = 1.0 / math.sqrt(rows * nty * cols * ntx)
+    nb = (nty * ntx).bit_length() - 1
+    return pl.pallas_call(
+        functools.partial(post_kernel, nty, ntx, size, wide, factor),
+        out_shape=(
+            jax.ShapeDtypeStruct((rows, cols, chans), BF16),
+            jax.ShapeDtypeStruct((49, chans), F32),
+            jax.ShapeDtypeStruct((chans, hid), F32),
+            jax.ShapeDtypeStruct((hid, chans), F32),
         ),
         in_specs=[vmem] * 7,
-        out_specs=(vmem,) * 3,
+        out_specs=(vmem,) * 4,
         scratch_shapes=[
+            pltpu.VMEM((size, 128), F32),
+            pltpu.VMEM((104, 128), F32),
             pltpu.VMEM((padded, 128), F32),
             pltpu.VMEM((halves * 49 * 8, 128), F32),
             pltpu.VMEM((size, 128), BF16),
@@ -511,15 +588,6 @@
         name="post",
     )(grad_core, *strips(grad_core), xpad, cotangent, taps, sums_in)
 
-    factor = 1.0 / math.sqrt(rows * nty * cols * ntx)
-    total_expand = jnp.concatenate([sums[k * chans : (k + 1) * chans] for k in range(wide)], axis=1)
-    base = wide * chans
-    total_reduce = jnp.concatenate(
-        [sums[base + k * hid : base + (k + 1) * hid] for k in range(halves)], axis=1
-    )
-    total_dw = jnp.concatenate([dsum[k * 49 : (k + 1) * 49] for k in range(halves)], axis=1)
-    return (out, total_dw * factor, total_expand * factor, total_reduce * factor)
-
 
 def solution(mesh):
     placed = (P("ty", "tx", None), P("ty", "tx", None), P("ty", "tx")) + (P(),) * 8

time: 141 us -> 110 us (0.78)
  matrix products: 17.4 us -> 0 us
  other arithmetic: 16.8 us -> 0 us
  Pallas kernels: 87.6 us -> 96.3 us
  local copies, waits for them, and re-layouts: 17.9 us -> 12.5 us
    dot_general x5 -> x0, matrix products: 17.4 us -> none  [the longest x1 6.77 us: branch_back(): dhid = jnp.dot(go_vals, w_reduce.T, preferred_element_type=F32)]
    pallas_call x1 -> x2, Pallas kernels: 60.4 us -> 73.3 us  [the longest x1 59.3 us: body(): pl.pallas_call(functools.partial(post_kernel, nty, ntx, size, wide, facto...]
    convert_element_type x5 -> x0, other arithmetic: 8.8 us -> none  [the longest x1 3.1 us: branch_back(): normed = (nhat * ln_gain + ln_bias).astype(BF16)]
    reduce_sum x2 -> x0, other arithmetic: 5.18 us -> none  [the longest x1 2.79 us: branch_back(): rstd = lax.rsqrt(jnp.mean(center * center, axis=-1, keepdims=True) + 1e-06)]
    pallas_call x1, Pallas kernels: 27.3 us -> 23 us  [body(): pl.pallas_call(functools.partial(pre_kernel, nty, ntx), out_shape=(jax.Sh...]
    unnamed x43 -> x30, local copies, waits for them, and re-layouts: 13 us -> 9.86 us
    mul x3 -> x0, other arithmetic: 2.81 us -> none  [the longest x1 1.12 us: body(): total_expand * factor]
where the time goes in v2:
time: 110 us
  Pallas kernels  96.3 us (88%)
  local copies, waits for them, and re-layouts  12.5 us (11%)
    pallas_call x1, Pallas kernels, body(): pl.pallas_call(functools.partial(post_kernel, nty, ntx, size, wide, facto...  59.3 us
    pallas_call x1, Pallas kernels, body(): pl.pallas_call(functools.partial(pre_kernel, nty, ntx), out_shape=(jax.Sh...  23 us
    pallas_call x1, Pallas kernels, body(): pl.pallas_call(mid_kernel, grid=(rows // TILE,), out_shape=(jax.ShapeDtyp...  14 us
    unnamed x30, local copies, waits for them, and re-layouts  9.86 us

profile of v2, /device:TPU:0, one launch (start us, length us, event | category | flops | bytes accessed | tf_op | source)
XLA Modules:
  0.0 109.7 jit_solution(8396873922236453417)
XLA Ops:
  0.6 0.0 copy-start.6
  0.6 0.0 copy-start.7
  0.7 0.0 copy-start.8
  0.7 0.0 copy-start.9
  0.7 0.0 copy-start.10
  0.7 0.0 copy-start.11
  0.7 0.0 copy-start.12
  0.7 0.9 reshape.29
  1.7 1.1 %fusion = (bf16[64,3,256]{2,1,0:T(4,128)(2,1)S(1)}, bf16[64,3,256]{2,1,0:T(4,128)(2,1)S(1)}) fusion(bf16[64,48,256]{2,1,0:T(8,128)(2,1)} %block.1), kind=kLoop, calls=%fused_computation.5 | loop fusion | bytes 393216 | tf_op jit(solution)/shard_map/slice | solution.py:423
  2.8 0.0 copy-start.2
  2.8 1.4 %copy-done.2 = bf16[64,48,256]{2,1,0:T(8,128)(2,1)S(1)} copy-done((bf16[64,48,256]{2,1,0:T(8,128)(2,1)S(1)}, bf16[64,48,256]{2,1,0:T(8,128)(2,1)}, u32[]{:S(2)}) %copy-start.2) | copy-done | bytes 1572888
  4.2 0.7 copy-done.5
  4.9 23.0 %pre.1 = (f32[64,48,256]{2,1,0:T(8,128)S(1)}, f32[8960,128]{1,0:T(8,128)S(1)}) custom-call(bf16[64,48,256]{2,1,0:T(8,128)(2,1)S(1)} %copy-done.2, bf16[3,64,256]{2,1,0:T(8,128)(2,1)S(1)} %get-tuple-element.17.left, bf16[3,64,256]{2,1,0:T(8,128)(2,1)S(1)} %get-tuple-element.16.right, f32[98,128]{1,0:T(8,128)S(1)} %reshape.30.taps, f32[2,128]{1,0:T(2,128)S(1)} %bitcast.16), custom_call_target="tpu_custom_call" | custom-call | flops 77070336 | bytes 16777216 | tf_op jit(solution)/shard_map/pre/pallas_call | solution.py:508
  27.9 0.0 copy-start.1
  28.0 2.1 %copy-done.1 = f32[8960,128]{1,0:T(8,128)} copy-done((f32[8960,128]{1,0:T(8,128)}, f32[8960,128]{1,0:T(8,128)S(1)}, u32[]{:S(2)}) %copy-start.1) | copy-done | bytes 4587544
  30.0 0.0 copy-done.6
  30.1 0.0 copy-done.7
  30.1 0.0 copy-done.8
  30.1 0.0 copy-done.9
  30.1 0.0 copy-done.10
  30.1 0.0 copy-done.11
  30.1 0.0 copy-done.12
  30.1 14.0 %mid.1 = (bf16[64,48,256]{2,1,0:T(8,128)(2,1)S(1)}, f32[4096,128]{1,0:T(8,128)S(1)}) custom-call(f32[64,48,256]{2,1,0:T(8,128)S(1)} %get-tuple-element.8.pre, bf16[64,48,256]{2,1,0:T(8,128)(2,1)S(1)} %copy-done.4, s32[4,3]{1,0:T(4,128)S(1)} %copy-done.9, f32[1,256]{1,0:T(1,128)S(1)} %bitcast.18, f32[1,256]{1,0:T(1,128)S(1)} %bitcast.19, ...), custom_call_target="tpu_custom_call" | custom-call | flops 8053063680 | bytes 12582912 | tf_op jit(solution)/shard_map/mid/pallas_call | solution.py:537
  44.1 0.0 copy-start.3
  44.2 1.4 %copy-done.3 = f32[4096,128]{1,0:T(8,128)} copy-done((f32[4096,128]{1,0:T(8,128)}, f32[4096,128]{1,0:T(8,128)S(1)}, u32[]{:S(2)}) %copy-start.3) | copy-done | bytes 2097176
  45.5 0.6 copy.23
  46.1 0.6 copy-done
  46.7 59.3 %post.1 = (bf16[64,48,256]{2,1,0:T(8,128)(2,1)S(1)}, f32[49,256]{1,0:T(8,128)S(1)}, f32[256,1024]{1,0:T(8,128)S(1)}, f32[1024,256]{1,0:T(8,128)S(1)}) custom-call(bf16[64,48,256]{2,1,0:T(8,128)(2,1)} %copy-done, bf16[3,64,256]{2,1,0:T(8,128)(2,1)S(1)} %get-tuple-element.13.left, bf16[3,64,256]{2,1,0:T(8,128)(2,1)S(1)} %get-tuple-element.12.right, ...), custom_call_target="tpu_custom_call" | custom-call | flops 154140672 | bytes 25165824 | tf_op jit(solution)/shard_map/post/pallas_call | solution.py:558
  105.9 1.1 %copy.35 = bf16[64,48,256]{2,1,0:T(8,128)(2,1)} copy(bf16[64,48,256]{2,1,0:T(8,128)(2,1)S(1)} %get-tuple-element.22) | data formatting | bytes 3145728
  107.1 0.6 copy.36
  107.7 1.0 copy.37
  108.7 1.0 copy.38
  (8 shorter events, 0.1 us)
Async XLA Ops:
  0.6 29.4 %copy-start.6 = (bf16[256,1024]{1,0:T(8,128)(2,1)S(1)}, bf16[256,1024]{1,0:T(8,128)(2,1)}, u32[]{:S(2)}) copy-start(bf16[256,1024]{1,0:T(8,128)(2,1)} %w_expand.1) | copy-start | bytes 1572868
  0.6 29.4 %copy-start.7 = (bf16[1024,256]{1,0:T(8,128)(2,1)S(1)}, bf16[1024,256]{1,0:T(8,128)(2,1)}, u32[]{:S(2)}) copy-start(bf16[1024,256]{1,0:T(8,128)(2,1)} %w_reduce.1) | copy-start | bytes 1572868
  0.7 29.4 %copy-start.8 = (f32[1024]{0:T(1024)S(1)}, f32[1024]{0:T(1024)}, u32[]{:S(2)}) copy-start(f32[1024]{0:T(1024)} %param.19) | copy-start | bytes 12292
  0.7 29.4 %copy-start.9 = (s32[4,3]{1,0:T(4,128)S(1)}, s32[4,3]{1,0:T(4,128)}, u32[]{:S(2)}) copy-start(s32[4,3]{1,0:T(4,128)} %tissue.1) | copy-start | bytes 148
  0.7 29.4 %copy-start.10 = (f32[256]{0:T(256)S(1)}, f32[256]{0:T(256)}, u32[]{:S(2)}) copy-start(f32[256]{0:T(256)} %param.16) | copy-start | bytes 3076
  0.7 29.4 %copy-start.11 = (f32[256]{0:T(256)S(1)}, f32[256]{0:T(256)}, u32[]{:S(2)}) copy-start(f32[256]{0:T(256)} %param.17) | copy-start | bytes 3076
  0.7 29.4 %copy-start.12 = (f32[256]{0:T(256)S(1)}, f32[256]{0:T(256)}, u32[]{:S(2)}) copy-start(f32[256]{0:T(256)} %param.21) | copy-start | bytes 3076
  2.8 1.4 %copy-start.2 = (bf16[64,48,256]{2,1,0:T(8,128)(2,1)S(1)}, bf16[64,48,256]{2,1,0:T(8,128)(2,1)}, u32[]{:S(2)}) copy-start(bf16[64,48,256]{2,1,0:T(8,128)(2,1)} %block.1) | copy-start | bytes 4718596
  4.2 0.7 copy-start.5
  4.9 25.2 %copy-start.4 = (bf16[64,48,256]{2,1,0:T(8,128)(2,1)S(1)}, bf16[64,48,256]{2,1,0:T(8,128)(2,1)}, u32[]{:S(2)}) copy-start(bf16[64,48,256]{2,1,0:T(8,128)(2,1)} %cot.3) | copy-start | bytes 4718596
  27.9 2.1 %copy-start.1 = (f32[8960,128]{1,0:T(8,128)}, f32[8960,128]{1,0:T(8,128)S(1)}, u32[]{:S(2)}) copy-start(f32[8960,128]{1,0:T(8,128)S(1)} %get-tuple-element.10.xblock_pad) | copy-start | bytes 13762564
  44.1 1.4 %copy-start.3 = (f32[4096,128]{1,0:T(8,128)}, f32[4096,128]{1,0:T(8,128)S(1)}, u32[]{:S(2)}) copy-start(f32[4096,128]{1,0:T(8,128)S(1)} %get-tuple-element.11.sums_in) | copy-start | bytes 6291460
  45.5 1.1 %copy-start = (bf16[64,48,256]{2,1,0:T(8,128)(2,1)}, bf16[64,48,256]{2,1,0:T(8,128)(2,1)S(1)}, u32[]{:S(2)}) copy-start(bf16[64,48,256]{2,1,0:T(8,128)(2,1)S(1)} %get-tuple-element.9.block) | copy-start | bytes 4718596

commit v3 on v2

--- a/solution.py
+++ b/solution.py
@@ -247,9 +247,6 @@
     pl.semaphore_wait(barrier, count + nb)
     halo.start()
 
-    lows = [jnp.int32(0)]
-    for k in range(nb):
-        lows.append(lows[k] + mine(k) * (size >> (k + 1)))
 
     def by_chunk(length, fn):
         step = min(length, 128)
@@ -260,64 +257,76 @@
 
         lax.fori_loop(0, length // step, go, 0)
 
-    def rs_copy(k):
-        length = size >> (k + 1)
-        away = pl.multiple_of(lows[k] + (1 - mine(k)) * length, 16)
-        return pltpu.make_async_remote_copy(
-            src_ref=ssend.at[pl.ds(away, length)],
-            dst_ref=srecv.at[pl.ds(size - 2 * length, length)],
-            send_sem=s_send.at[k],
-            recv_sem=s_recv.at[k],
-            device_id=partner(k),
-            device_id_type=MESH,
-        )
-
-    def rs_start(k):
-        length = size >> (k + 1)
-        away = lows[k] + (1 - mine(k)) * length
-        source = sums_in if k == 0 else sums
-
-        def cast(i, step):
-            at = pl.multiple_of(away + i, 16)
-            ssend[pl.ds(at, step), :] = source[pl.ds(at, step), :].astype(BF16)
-
-        by_chunk(length, cast)
-        rs_copy(k).start()
-
-    def rs_end(k):
-        length = size >> (k + 1)
-        source = sums_in if k == 0 else sums
-        rs_copy(k).wait()
-
-        def add(i, step):
-            at = pl.multiple_of(lows[k + 1] + i, 16)
-            got = srecv[pl.ds(pl.multiple_of(size - 2 * length + i, 16), step), :]
-            sums[pl.ds(at, step), :] = source[pl.ds(at, step), :] + got.astype(F32)
-
-        by_chunk(length, add)
-
-    def ag_copy(k):
-        length = size >> (k + 1)
-        at = pl.multiple_of(lows[k + 1], 16)
-        return pltpu.make_async_remote_copy(
-            src_ref=gathered.at[pl.ds(at, length)],
-            dst_ref=gathered.at[pl.ds(at, length)],
-            send_sem=s_send.at[nb + k],
-            recv_sem=s_recv.at[nb + k],
-            device_id=partner(k),
-            device_id_type=MESH,
-        )
-
-    def ag_start(k):
-        if k == nb - 1:
-            length = size >> nb
+    def chain(base, size, order, sem):
+        lows = [jnp.int32(base)]
+        for k in range(nb):
+            lows.append(lows[k] + mine(order[k]) * (size >> (k + 1)))
+
+        def rs_copy(k):
+            length = size >> (k + 1)
+            away = pl.multiple_of(lows[k] + (1 - mine(order[k])) * length, 16)
+            return pltpu.make_async_remote_copy(
+                src_ref=ssend.at[pl.ds(away, length)],
+                dst_ref=srecv.at[pl.ds(base + size - 2 * length, length)],
+                send_sem=s_send.at[sem + k],
+                recv_sem=s_recv.at[sem + k],
+                device_id=partner(order[k]),
+                device_id_type=MESH,
+            )
+
+        def rs_start(k):
+            length = size >> (k + 1)
+            away = lows[k] + (1 - mine(order[k])) * length
+            source = sums_in if k == 0 else sums
 
             def cast(i, step):
-                at = pl.multiple_of(lows[nb] + i, 16)
-                gathered[pl.ds(at, step), :] = sums[pl.ds(at, step), :].astype(BF16)
+                at = pl.multiple_of(away + i, 16)
+                ssend[pl.ds(at, step), :] = source[pl.ds(at, step), :].astype(BF16)
 
             by_chunk(length, cast)
-        ag_copy(k).start()
+            rs_copy(k).start()
+
+        def rs_end(k):
+            length = size >> (k + 1)
+            source = sums_in if k == 0 else sums
+            rs_copy(k).wait()
+
+            def add(i, step):
+                at = pl.multiple_of(lows[k + 1] + i, 16)
+                got = srecv[pl.ds(pl.multiple_of(base + size - 2 * length + i, 16), step), :]
+                sums[pl.ds(at, step), :] = source[pl.ds(at, step), :] + got.astype(F32)
+
+            by_chunk(length, add)
+
+        def ag_copy(k):
+            length = size >> (k + 1)
+            at = pl.multiple_of(lows[k + 1], 16)
+            return pltpu.make_async_remote_copy(
+                src_ref=gathered.at[pl.ds(at, length)],
+                dst_ref=gathered.at[pl.ds(at, length)],
+                send_sem=s_send.at[sem + nb + k],
+                recv_sem=s_recv.at[sem + nb + k],
+                device_id=partner(order[k]),
+                device_id_type=MESH,
+            )
+
+        def ag_start(k):
+            if k == nb - 1:
+                length = size >> nb
+
+                def cast(i, step):
+                    at = pl.multiple_of(lows[nb] + i, 16)
+                    gathered[pl.ds(at, step), :] = sums[pl.ds(at, step), :].astype(BF16)
+
+                by_chunk(length, cast)
+            ag_copy(k).start()
+
+        events = []
+        for k in range(nb):
+            events.append((functools.partial(rs_start, k), functools.partial(rs_end, k)))
+        for k in reversed(range(nb)):
+            events.append((functools.partial(ag_start, k), ag_copy(k).wait))
+        return events
 
     def d_copy(k):
         return pltpu.make_async_remote_copy(
@@ -329,11 +338,14 @@
             device_id_type=MESH,
         )
 
-    events = []
-    for k in range(nb):
-        events.append((functools.partial(rs_start, k), functools.partial(rs_end, k)))
-    for k in reversed(range(nb)):
-        events.append((functools.partial(ag_start, k), ag_copy(k).wait))
+    first = list(range(nb))
+    second = first[:1] + first[1:3][::-1] + first[3:]
+    events = [
+        (functools.partial(both, one[0], two[0]), functools.partial(both, one[1], two[1]))
+        for one, two in zip(
+            chain(0, size // 2, first, 0), chain(size // 2, size // 2, second, 2 * nb)
+        )
+    ]
     d_events = [(d_copy(k).start, functools.partial(lambda k: d_end(k), k)) for k in range(nb)]
 
     def d_end(k):
@@ -414,6 +426,11 @@
         reduce[k * 128 : (k + 1) * 128, :] = jnp.transpose(part)
     for h in range(halves):
         dw[:, h * 128 : (h + 1) * 128] = dsum[h * 49 : (h + 1) * 49, :] * factor
+
+
+def both(one, two):
+    one()
+    two()
 
 
 def strips(block):
@@ -522,7 +539,7 @@
     )(block_input, *strips(block_input), taps, dw_bias.reshape(halves, 128))
 
     wide = hid // 128
-    unit = nty * ntx * 16
+    unit = nty * ntx * 32
     size = -(-2 * wide * chans // unit) * unit
     one = lambda array: pl.BlockSpec(array.shape, lambda i: (0,) * array.ndim)
     per_tile = pl.BlockSpec((TILE, cols, chans), lambda i: (i, 0, 0))
@@ -575,8 +592,8 @@
             pltpu.VMEM((size, 128), BF16),
             pltpu.VMEM((nb, 104, 128), F32),
             pltpu.VMEM((nb, 104, 128), F32),
-            pltpu.SemaphoreType.DMA((2 * nb,)),
-            pltpu.SemaphoreType.DMA((2 * nb,)),
+            pltpu.SemaphoreType.DMA((4 * nb,)),
+            pltpu.SemaphoreType.DMA((4 * nb,)),
             pltpu.SemaphoreType.DMA((nb,)),
             pltpu.SemaphoreType.DMA((nb,)),
         ]

time: 110 us -> 105 us (0.955)
  Pallas kernels: 96.3 us -> 91.3 us
    pallas_call x1, Pallas kernels: 59.3 us -> 54.3 us  [body(): pl.pallas_call(functools.partial(post_kernel, nty, ntx, size, wide, facto...]
where the time goes in v3:
time: 105 us
  Pallas kernels  91.3 us (87%)
  local copies, waits for them, and re-layouts  12.5 us (12%)
    pallas_call x1, Pallas kernels, body(): pl.pallas_call(functools.partial(post_kernel, nty, ntx, size, wide, facto...  54.3 us
    pallas_call x1, Pallas kernels, body(): pl.pallas_call(functools.partial(pre_kernel, nty, ntx), out_shape=(jax.Sh...  23 us
    pallas_call x1, Pallas kernels, body(): pl.pallas_call(mid_kernel, grid=(rows // TILE,), out_shape=(jax.ShapeDtyp...  14 us
    unnamed x30, local copies, waits for them, and re-layouts  9.86 us

profile of v3, /device:TPU:0, one launch (start us, length us, event | category | flops | bytes accessed | tf_op | source)
XLA Modules:
  0.0 104.6 jit_solution(6375519051862060203)
XLA Ops:
  0.6 0.0 copy-start.6
  0.6 0.0 copy-start.7
  0.7 0.0 copy-start.8
  0.7 0.0 copy-start.9
  0.7 0.0 copy-start.10
  0.7 0.0 copy-start.11
  0.7 0.0 copy-start.12
  0.7 0.9 reshape.29
  1.7 1.1 %fusion = (bf16[64,3,256]{2,1,0:T(4,128)(2,1)S(1)}, bf16[64,3,256]{2,1,0:T(4,128)(2,1)S(1)}) fusion(bf16[64,48,256]{2,1,0:T(8,128)(2,1)} %block.1), kind=kLoop, calls=%fused_computation.5 | loop fusion | bytes 393216 | tf_op jit(solution)/shard_map/slice | solution.py:440
  2.8 0.0 copy-start.2
  2.8 1.4 %copy-done.2 = bf16[64,48,256]{2,1,0:T(8,128)(2,1)S(1)} copy-done((bf16[64,48,256]{2,1,0:T(8,128)(2,1)S(1)}, bf16[64,48,256]{2,1,0:T(8,128)(2,1)}, u32[]{:S(2)}) %copy-start.2) | copy-done | bytes 1572888
  4.2 0.7 copy-done.5
  4.9 23.0 %pre.1 = (f32[64,48,256]{2,1,0:T(8,128)S(1)}, f32[8960,128]{1,0:T(8,128)S(1)}) custom-call(bf16[64,48,256]{2,1,0:T(8,128)(2,1)S(1)} %copy-done.2, bf16[3,64,256]{2,1,0:T(8,128)(2,1)S(1)} %get-tuple-element.17.left, bf16[3,64,256]{2,1,0:T(8,128)(2,1)S(1)} %get-tuple-element.16.right, f32[98,128]{1,0:T(8,128)S(1)} %reshape.30.taps, f32[2,128]{1,0:T(2,128)S(1)} %bitcast.16), custom_call_target="tpu_custom_call" | custom-call | flops 77070336 | bytes 16777216 | tf_op jit(solution)/shard_map/pre/pallas_call | solution.py:525
  27.9 0.0 copy-start.1
  28.0 2.1 %copy-done.1 = f32[8960,128]{1,0:T(8,128)} copy-done((f32[8960,128]{1,0:T(8,128)}, f32[8960,128]{1,0:T(8,128)S(1)}, u32[]{:S(2)}) %copy-start.1) | copy-done | bytes 4587544
  30.0 0.0 copy-done.6
  30.1 0.0 copy-done.7
  30.1 0.0 copy-done.8
  30.1 0.0 copy-done.9
  30.1 0.0 copy-done.10
  30.1 0.0 copy-done.11
  30.1 0.0 copy-done.12
  30.1 14.0 %mid.1 = (bf16[64,48,256]{2,1,0:T(8,128)(2,1)S(1)}, f32[4096,128]{1,0:T(8,128)S(1)}) custom-call(f32[64,48,256]{2,1,0:T(8,128)S(1)} %get-tuple-element.8.pre, bf16[64,48,256]{2,1,0:T(8,128)(2,1)S(1)} %copy-done.4, s32[4,3]{1,0:T(4,128)S(1)} %copy-done.9, f32[1,256]{1,0:T(1,128)S(1)} %bitcast.18, f32[1,256]{1,0:T(1,128)S(1)} %bitcast.19, ...), custom_call_target="tpu_custom_call" | custom-call | flops 8053063680 | bytes 12582912 | tf_op jit(solution)/shard_map/mid/pallas_call | solution.py:554
  44.1 0.0 copy-start.3
  44.2 1.4 %copy-done.3 = f32[4096,128]{1,0:T(8,128)} copy-done((f32[4096,128]{1,0:T(8,128)}, f32[4096,128]{1,0:T(8,128)S(1)}, u32[]{:S(2)}) %copy-start.3) | copy-done | bytes 2097176
  45.5 0.6 copy.23
  46.1 0.6 copy-done
  46.7 54.3 %post.1 = (bf16[64,48,256]{2,1,0:T(8,128)(2,1)S(1)}, f32[49,256]{1,0:T(8,128)S(1)}, f32[256,1024]{1,0:T(8,128)S(1)}, f32[1024,256]{1,0:T(8,128)S(1)}) custom-call(bf16[64,48,256]{2,1,0:T(8,128)(2,1)} %copy-done, bf16[3,64,256]{2,1,0:T(8,128)(2,1)S(1)} %get-tuple-element.13.left, bf16[3,64,256]{2,1,0:T(8,128)(2,1)S(1)} %get-tuple-element.12.right, ...), custom_call_target="tpu_custom_call" | custom-call | flops 154140672 | bytes 25165824 | tf_op jit(solution)/shard_map/post/pallas_call | solution.py:575
  100.9 1.1 %copy.35 = bf16[64,48,256]{2,1,0:T(8,128)(2,1)} copy(bf16[64,48,256]{2,1,0:T(8,128)(2,1)S(1)} %get-tuple-element.22) | data formatting | bytes 3145728
  102.1 0.6 copy.36
  102.7 1.0 copy.37
  103.7 1.0 copy.38
  (8 shorter events, 0.1 us)
Async XLA Ops:
  0.6 29.4 %copy-start.6 = (bf16[256,1024]{1,0:T(8,128)(2,1)S(1)}, bf16[256,1024]{1,0:T(8,128)(2,1)}, u32[]{:S(2)}) copy-start(bf16[256,1024]{1,0:T(8,128)(2,1)} %w_expand.1) | copy-start | bytes 1572868
  0.6 29.4 %copy-start.7 = (bf16[1024,256]{1,0:T(8,128)(2,1)S(1)}, bf16[1024,256]{1,0:T(8,128)(2,1)}, u32[]{:S(2)}) copy-start(bf16[1024,256]{1,0:T(8,128)(2,1)} %w_reduce.1) | copy-start | bytes 1572868
  0.7 29.4 %copy-start.8 = (f32[1024]{0:T(1024)S(1)}, f32[1024]{0:T(1024)}, u32[]{:S(2)}) copy-start(f32[1024]{0:T(1024)} %param.19) | copy-start | bytes 12292
  0.7 29.4 %copy-start.9 = (s32[4,3]{1,0:T(4,128)S(1)}, s32[4,3]{1,0:T(4,128)}, u32[]{:S(2)}) copy-start(s32[4,3]{1,0:T(4,128)} %tissue.1) | copy-start | bytes 148
  0.7 29.4 %copy-start.10 = (f32[256]{0:T(256)S(1)}, f32[256]{0:T(256)}, u32[]{:S(2)}) copy-start(f32[256]{0:T(256)} %param.16) | copy-start | bytes 3076
  0.7 29.4 %copy-start.11 = (f32[256]{0:T(256)S(1)}, f32[256]{0:T(256)}, u32[]{:S(2)}) copy-start(f32[256]{0:T(256)} %param.17) | copy-start | bytes 3076
  0.7 29.4 %copy-start.12 = (f32[256]{0:T(256)S(1)}, f32[256]{0:T(256)}, u32[]{:S(2)}) copy-start(f32[256]{0:T(256)} %param.21) | copy-start | bytes 3076
  2.8 1.4 %copy-start.2 = (bf16[64,48,256]{2,1,0:T(8,128)(2,1)S(1)}, bf16[64,48,256]{2,1,0:T(8,128)(2,1)}, u32[]{:S(2)}) copy-start(bf16[64,48,256]{2,1,0:T(8,128)(2,1)} %block.1) | copy-start | bytes 4718596
  4.2 0.7 copy-start.5
  4.9 25.2 %copy-start.4 = (bf16[64,48,256]{2,1,0:T(8,128)(2,1)S(1)}, bf16[64,48,256]{2,1,0:T(8,128)(2,1)}, u32[]{:S(2)}) copy-start(bf16[64,48,256]{2,1,0:T(8,128)(2,1)} %cot.3) | copy-start | bytes 4718596
  27.9 2.1 %copy-start.1 = (f32[8960,128]{1,0:T(8,128)}, f32[8960,128]{1,0:T(8,128)S(1)}, u32[]{:S(2)}) copy-start(f32[8960,128]{1,0:T(8,128)S(1)} %get-tuple-element.10.xblock_pad) | copy-start | bytes 13762564
  44.1 1.4 %copy-start.3 = (f32[4096,128]{1,0:T(8,128)}, f32[4096,128]{1,0:T(8,128)S(1)}, u32[]{:S(2)}) copy-start(f32[4096,128]{1,0:T(8,128)S(1)} %get-tuple-element.11.sums_in) | copy-start | bytes 6291460
  45.5 1.1 %copy-start = (bf16[64,48,256]{2,1,0:T(8,128)(2,1)}, bf16[64,48,256]{2,1,0:T(8,128)(2,1)S(1)}, u32[]{:S(2)}) copy-start(bf16[64,48,256]{2,1,0:T(8,128)(2,1)S(1)} %get-tuple-element.9.block) | copy-start | bytes 4718596

commit v4 on v3

--- a/solution.py
+++ b/solution.py
@@ -532,7 +532,7 @@
         out_specs=(vmem, vmem),
         scratch_shapes=halo_bufs(cols, rows, chans),
         compiler_params=pltpu.CompilerParams(
-            collective_id=0, has_side_effects=True, vmem_limit_bytes=40 << 20
+            collective_id=0, has_side_effects=True, vmem_limit_bytes=24 << 20
         ),
         cost_estimate=pl.CostEstimate(flops=flops, bytes_accessed=16 << 20, transcendentals=0),
         name="pre",
@@ -561,7 +561,7 @@
         in_specs=[per_tile, per_tile, pl.BlockSpec(memory_space=pltpu.SMEM)]
         + [one(array) for array in whole],
         out_specs=(per_tile, pl.BlockSpec((size, 128), lambda i: (0, 0))),
-        compiler_params=pltpu.CompilerParams(vmem_limit_bytes=44 << 20),
+        compiler_params=pltpu.CompilerParams(vmem_limit_bytes=36 << 20),
         cost_estimate=pl.CostEstimate(
             flops=10 * rows * cols * chans * hid,
             bytes_accessed=12 << 20,
@@ -599,7 +599,7 @@
         ]
         + halo_bufs(cols, rows, chans),
         compiler_params=pltpu.CompilerParams(
-            collective_id=1, has_side_effects=True, vmem_limit_bytes=50 << 20
+            collective_id=1, has_side_effects=True, vmem_limit_bytes=36 << 20
         ),
         cost_estimate=pl.CostEstimate(flops=2 * flops, bytes_accessed=24 << 20, transcendentals=0),
         name="post",

time: 105 us -> 97.2 us (0.926)
  local copies, waits for them, and re-layouts: 12.5 us -> 8.49 us
  Pallas kernels: 91.3 us -> 87.7 us
    unnamed x30 -> x24, local copies, waits for them, and re-layouts: 9.86 us -> 5.82 us
    pallas_call x1, Pallas kernels: 54.3 us -> 51.2 us  [body(): pl.pallas_call(functools.partial(post_kernel, nty, ntx, size, wide, facto...]
where the time goes in v4:
time: 97.2 us; the launch traced here: 97 us
  Pallas kernels  87.7 us (90%)
  local copies, waits for them, and re-layouts  8.49 us (9%)
    pallas_call x1, Pallas kernels, body(): pl.pallas_call(functools.partial(post_kernel, nty, ntx, size, wide, facto...  51.2 us
    pallas_call x1, Pallas kernels, body(): pl.pallas_call(functools.partial(pre_kernel, nty, ntx), out_shape=(jax.Sh...  22.5 us
    pallas_call x1, Pallas kernels, body(): pl.pallas_call(mid_kernel, grid=(rows // TILE,), out_shape=(jax.ShapeDtyp...  14 us
    unnamed x24, local copies, waits for them, and re-layouts  5.82 us

profile of v4, /device:TPU:0, one launch (start us, length us, event | category | flops | bytes accessed | tf_op | source)
XLA Modules:
  0.0 97.0 jit_solution(16476295709212289365)
XLA Ops:
  0.6 0.0 copy-start.3
  0.6 0.0 copy-start.4
  0.7 0.0 copy-start.5
  0.7 0.0 copy-start.6
  0.7 0.0 copy-start.7
  0.7 0.0 copy-start.8
  0.7 0.0 copy-start.9
  0.7 0.9 reshape.29
  1.7 1.1 %fusion = (bf16[64,3,256]{2,1,0:T(4,128)(2,1)S(1)}, bf16[64,3,256]{2,1,0:T(4,128)(2,1)S(1)}) fusion(bf16[64,48,256]{2,1,0:T(8,128)(2,1)} %block.1), kind=kLoop, calls=%fused_computation.5 | loop fusion | bytes 393216 | tf_op jit(solution)/shard_map/slice | solution.py:440
  2.8 0.0 copy-start
  2.8 1.4 %copy-done = bf16[64,48,256]{2,1,0:T(8,128)(2,1)S(1)} copy-done((bf16[64,48,256]{2,1,0:T(8,128)(2,1)S(1)}, bf16[64,48,256]{2,1,0:T(8,128)(2,1)}, u32[]{:S(2)}) %copy-start) | copy-done | bytes 1572888
  4.2 0.0 copy-start.2
  4.2 0.7 copy-done.2
  4.9 0.0 copy-start.1
  4.9 22.5 %pre.1 = (f32[64,48,256]{2,1,0:T(8,128)S(1)}, f32[8960,128]{1,0:T(8,128)S(1)}) custom-call(bf16[64,48,256]{2,1,0:T(8,128)(2,1)S(1)} %copy-done, bf16[3,64,256]{2,1,0:T(8,128)(2,1)S(1)} %get-tuple-element.17.left, bf16[3,64,256]{2,1,0:T(8,128)(2,1)S(1)} %get-tuple-element.16.right, f32[98,128]{1,0:T(8,128)S(1)} %reshape.30.taps, f32[2,128]{1,0:T(2,128)S(1)} %bitcast.16), custom_call_target="tpu_custom_call" | custom-call | flops 77070336 | bytes 16777216 | tf_op jit(solution)/shard_map/pre/pallas_call | solution.py:525
  27.4 0.0 copy-done.3
  27.4 0.0 copy-done.4
  27.5 0.0 copy-done.5
  27.5 0.0 copy-done.6
  27.5 0.0 copy-done.7
  27.5 0.0 copy-done.8
  27.5 0.0 copy-done.9
  27.5 0.0 copy-done.1
  27.5 14.0 %mid.1 = (bf16[64,48,256]{2,1,0:T(8,128)(2,1)S(1)}, f32[4096,128]{1,0:T(8,128)S(1)}) custom-call(f32[64,48,256]{2,1,0:T(8,128)S(1)} %get-tuple-element.8.pre, bf16[64,48,256]{2,1,0:T(8,128)(2,1)S(1)} %copy-done.1, s32[4,3]{1,0:T(4,128)S(1)} %copy-done.6, f32[1,256]{1,0:T(1,128)S(1)} %bitcast.18, f32[1,256]{1,0:T(1,128)S(1)} %bitcast.19, ...), custom_call_target="tpu_custom_call" | custom-call | flops 8053063680 | bytes 12582912 | tf_op jit(solution)/shard_map/mid/pallas_call | solution.py:554
  41.5 0.6 copy.23
  42.1 51.2 %post.1 = (bf16[64,48,256]{2,1,0:T(8,128)(2,1)S(1)}, f32[49,256]{1,0:T(8,128)S(1)}, f32[256,1024]{1,0:T(8,128)S(1)}, f32[1024,256]{1,0:T(8,128)S(1)}) custom-call(bf16[64,48,256]{2,1,0:T(8,128)(2,1)S(1)} %get-tuple-element.9.block, bf16[3,64,256]{2,1,0:T(8,128)(2,1)S(1)} %get-tuple-element.13.left, bf16[3,64,256]{2,1,0:T(8,128)(2,1)S(1)} %get-tuple-element.12.right, ...), custom_call_target="tpu_custom_call" | custom-call | flops 154140672 | bytes 25165824 | tf_op jit(solution)/shard_map/post/pallas_call | solution.py:575
  93.3 1.1 %copy.35 = bf16[64,48,256]{2,1,0:T(8,128)(2,1)} copy(bf16[64,48,256]{2,1,0:T(8,128)(2,1)S(1)} %get-tuple-element.22) | data formatting | bytes 3145728
  94.4 0.6 copy.36
  95.1 1.0 copy.37
  96.0 1.0 copy.38
  (4 shorter events, 0.1 us)
Async XLA Ops:
  0.6 26.8 %copy-start.3 = (bf16[256,1024]{1,0:T(8,128)(2,1)S(1)}, bf16[256,1024]{1,0:T(8,128)(2,1)}, u32[]{:S(2)}) copy-start(bf16[256,1024]{1,0:T(8,128)(2,1)} %w_expand.1) | copy-start | bytes 1572868
  0.6 26.8 %copy-start.4 = (bf16[1024,256]{1,0:T(8,128)(2,1)S(1)}, bf16[1024,256]{1,0:T(8,128)(2,1)}, u32[]{:S(2)}) copy-start(bf16[1024,256]{1,0:T(8,128)(2,1)} %w_reduce.1) | copy-start | bytes 1572868
  0.7 26.8 %copy-start.5 = (f32[1024]{0:T(1024)S(1)}, f32[1024]{0:T(1024)}, u32[]{:S(2)}) copy-start(f32[1024]{0:T(1024)} %param.19) | copy-start | bytes 12292
  0.7 26.8 %copy-start.6 = (s32[4,3]{1,0:T(4,128)S(1)}, s32[4,3]{1,0:T(4,128)}, u32[]{:S(2)}) copy-start(s32[4,3]{1,0:T(4,128)} %tissue.1) | copy-start | bytes 148
  0.7 26.8 %copy-start.7 = (f32[256]{0:T(256)S(1)}, f32[256]{0:T(256)}, u32[]{:S(2)}) copy-start(f32[256]{0:T(256)} %param.16) | copy-start | bytes 3076
  0.7 26.8 %copy-start.8 = (f32[256]{0:T(256)S(1)}, f32[256]{0:T(256)}, u32[]{:S(2)}) copy-start(f32[256]{0:T(256)} %param.17) | copy-start | bytes 3076
  0.7 26.8 %copy-start.9 = (f32[256]{0:T(256)S(1)}, f32[256]{0:T(256)}, u32[]{:S(2)}) copy-start(f32[256]{0:T(256)} %param.21) | copy-start | bytes 3076
  2.8 1.4 %copy-start = (bf16[64,48,256]{2,1,0:T(8,128)(2,1)S(1)}, bf16[64,48,256]{2,1,0:T(8,128)(2,1)}, u32[]{:S(2)}) copy-start(bf16[64,48,256]{2,1,0:T(8,128)(2,1)} %block.1) | copy-start | bytes 4718596
  4.2 0.7 copy-start.2
  4.9 22.6 %copy-start.1 = (bf16[64,48,256]{2,1,0:T(8,128)(2,1)S(1)}, bf16[64,48,256]{2,1,0:T(8,128)(2,1)}, u32[]{:S(2)}) copy-start(bf16[64,48,256]{2,1,0:T(8,128)(2,1)} %cot.3) | copy-start | bytes 4718596
